TPU v7x, 128 devices: a whole 4x4x4 slice. The times are simulated.
128 devices in a mesh: node: 8 (over y, core), local: 16 (over z, x).
Axes of the slice: x: 4, y: 4, z: 4, core: 2. Of those that a mesh axis runs over, the one named last changes fastest.
Arguments:
- out_grad: bfloat16 [16384, 3584], P(('node', 'local')), may hold values from -6 to 6
- gates: bfloat16 [16384, 2], P(('node', 'local')), may hold values from 0.099609375 to 2
- expert_ids: int32 [16384, 2], P(('node', 'local')), may hold values from 0 to 31, as said below
- saved_pre: bfloat16 [128, 128, 12, 1024], P(('node', 'local')), may hold values from -6 to 6
- w_gate_up: bfloat16 [128, 3584, 1024], P(('node', 'local')), may hold values from -0.09375 to 0.09375
- w_down: bfloat16 [128, 512, 3584], P(('node', 'local')), may hold values from -0.125 to 0.125
Outputs:
- input_grad: bfloat16 [16384, 3584], P(('node', 'local'))
- gate_grad: float32 [16384, 2], P(('node', 'local'))
- down_grad: bfloat16 [128, 512, 3584], P(('node', 'local'))
Inputs may be any that keep to these rules, and one draw needn't show every extreme that they name: `expert_ids`: each token names 2 different experts, all of one node group (expert e belongs to group e // 4). Among the tokens of one device, at most 24 name experts of any one group and at most 12 name any one expert; on every device some group has exactly 24 tokens and some expert exactly 12.
All inputs are finite; a program needn't handle non-finite values.
Results may differ from a plain program's by a relative error of at most 0.0057.
Values may be sent and summed in bfloat16 or wider, within the bound.
A program may use at most 192 MiB of HBM per device.

v0:
```python
import jax
import jax.numpy as jnp
from jax import lax
from jax.sharding import PartitionSpec as P

FF = 2048


def expert_backward(rows, weights_here, saved, gate_up, down):
    hidden_units = down.shape[0]
    gate_pre = saved[:, :hidden_units].astype(jnp.float32)
    up_pre = saved[:, hidden_units:].astype(jnp.float32)
    sigma = jax.nn.sigmoid(gate_pre)
    activation = gate_pre * sigma
    hidden = activation * up_pre
    d_act = lax.dot_general(
        rows, down, (((1,), (1,)), ((), ())), preferred_element_type=jnp.float32
    )
    gate_part = jnp.sum(hidden * d_act, axis=-1).astype(jnp.bfloat16)
    scale = weights_here.astype(jnp.float32)[:, None]
    d_hidden = scale * d_act
    d_gate = d_hidden * up_pre * sigma * (1.0 + gate_pre * (1.0 - sigma))
    d_up = d_hidden * activation
    d_pre = jnp.concatenate([d_gate, d_up], axis=-1).astype(jnp.bfloat16)
    x_part = lax.dot_general(
        d_pre, gate_up, (((1,), (1,)), ((), ())), preferred_element_type=jnp.float32
    ).astype(jnp.bfloat16)
    weighted = (scale * hidden).astype(jnp.bfloat16)
    w_grad = lax.dot_general(
        weighted, rows, (((0,), (0,)), ((), ())), preferred_element_type=jnp.float32
    ).astype(jnp.bfloat16)
    return (x_part, gate_part, w_grad)


def body(out_grad, gates, expert_ids, saved_pre, w_gate_up, w_down):
    tok_count, width = out_grad.shape
    node_count = lax.axis_size("node")
    local_count = lax.axis_size("local")
    unit_count = node_count * local_count
    hidden_units = w_down.shape[1]
    slices_here = FF // hidden_units
    per_group = local_count // slices_here
    expert_count = node_count * per_group
    slot_cap = saved_pre.shape[2]
    expert_axis = jnp.arange(expert_count, dtype=jnp.int32)
    onehot = (expert_ids[:, :, None] == expert_axis).astype(jnp.int32)
    per_token = jnp.sum(onehot, axis=1)
    earlier = jnp.cumsum(per_token, axis=0) - per_token
    rank = jnp.sum(earlier[:, None, :] * onehot, axis=-1)
    token_axis = jnp.arange(tok_count, dtype=jnp.int32)
    padded_rows = jnp.concatenate([out_grad, jnp.zeros((1, width), jnp.bfloat16)], axis=0)
    saved = saved_pre[0].reshape(unit_count * slot_cap, 2 * hidden_units)
    gate_up = w_gate_up[0]
    down = w_down[0]
    owner_node = expert_ids // per_group
    member = expert_ids % per_group
    target = (owner_node * local_count + member * slices_here)[..., None] + jnp.arange(
        slices_here, dtype=jnp.int32
    )
    slot_pos = target * slot_cap + rank[..., None]
    slot_total = unit_count * slot_cap
    flat_pos = slot_pos.reshape(-1)
    token_table = (
        jnp.full((slot_total,), tok_count, jnp.int32)
        .at[flat_pos]
        .set(jnp.broadcast_to(token_axis[:, None, None], slot_pos.shape).reshape(-1))
    )
    gate_slots = (
        jnp.zeros((slot_total,), jnp.bfloat16)
        .at[flat_pos]
        .set(jnp.broadcast_to(gates[..., None], slot_pos.shape).reshape(-1))
    )
    outgoing = padded_rows[token_table].reshape(unit_count, slot_cap, width)
    rows_in, gates_in = (
        lax.all_to_all(outgoing, ("node", "local"), split_axis=0, concat_axis=0, tiled=True),
        lax.all_to_all(
            gate_slots.reshape(unit_count, slot_cap),
            ("node", "local"),
            split_axis=0,
            concat_axis=0,
            tiled=True,
        ),
    )
    x_part, gate_part, w_grad = expert_backward(
        rows_in.reshape(-1, width), gates_in.reshape(-1), saved, gate_up, down
    )
    back_rows, back_gates = (
        lax.all_to_all(
            x_part.reshape(unit_count, slot_cap, width),
            ("node", "local"),
            split_axis=0,
            concat_axis=0,
            tiled=True,
        ),
        lax.all_to_all(
            gate_part.reshape(unit_count, slot_cap),
            ("node", "local"),
            split_axis=0,
            concat_axis=0,
            tiled=True,
        ),
    )
    picked = back_rows.reshape(-1, width)[slot_pos.reshape(tok_count, -1)]
    input_grad = jnp.sum(picked.astype(jnp.float32), axis=1).astype(jnp.bfloat16)
    gate_grad = jnp.sum(back_gates.reshape(-1)[slot_pos].astype(jnp.float32), axis=-1)
    return (input_grad, gate_grad, w_grad[None])


def solution(mesh):
    in_specs = (
        P(("node", "local"), None),
        P(("node", "local"), None),
        P(("node", "local"), None),
        P(("node", "local"), None, None, None),
        P(("node", "local"), None, None),
        P(("node", "local"), None, None),
    )
    out_specs = (
        P(("node", "local"), None),
        P(("node", "local"), None),
        P(("node", "local"), None, None),
    )
    return jax.shard_map(body, mesh=mesh, in_specs=in_specs, out_specs=out_specs, check_vma=False)
```

profile of v0, /device:TPU:0, one launch (start us, length us, event | category | flops | bytes accessed | tf_op | source)
XLA Modules:
  0.0 602.4 jit_solution(6927882603836880737)
XLA Ops:
  0.6 0.7 fusion.20
  1.3 0.7 convert_reduce_fusion.1
  2.0 0.8 copy.39
  2.8 0.2 broadcast_in_dim.13
  3.0 0.1 reshape.237
  3.2 0.2 reduce_window_sum.11
  3.5 0.7 select_reduce_fusion
  4.2 0.2 copy.38
  4.4 0.2 add.163
  4.6 7.6 %scatter_custom_fusion = bf16[1536]{0:T(1024)(128)(2,1)S(1)} fusion(s32[1024]{0:T(1024)S(1)} %bitcast.25, bf16[1024]{0:T(1024)(128)(2,1)S(1)} %reshape.237, bf16[]{:T(256)} %constant.21.clone.1), kind=kCustom, calls=%fused_computation.45 | custom fusion | bytes 3074 | tf_op jit(solution)/shard_map/scatter | solution.py:71
  12.2 0.8 all_to_all.21
  12.9 11.1 %all-to-all-start = ((bf16[128,1,12]{2,1,0:T(2,128)(2,1)}), bf16[128,1,12]{2,1,0:T(2,128)(2,1)S(1)}, u32[]{:S(2)}, u32[]{:S(2)}) async-start(bf16[128,1,12]{2,1,0:T(2,128)(2,1)} %all_to_all.21), calls=%async_computation | async-start | bytes 131072 | tf_op jit(solution)/shard_map/all_to_all | solution.py:76
  24.1 0.2 reshape.245
  24.3 4.3 scatter_custom_fusion.1
  28.7 1.2 concatenate.7
  29.9 9.1 %gather_fusion = bf16[1536,3584]{1,0:T(8,128)(2,1)} fusion(bf16[129,3584]{1,0:T(8,128)(2,1)S(1)} %concatenate.7, s32[2048]{0:T(1024)S(1)} %pad_clamp_fusion), kind=kCustom, calls=%fused_computation | custom fusion | bytes 22026240 | tf_op jit(solution)/shard_map/gather | solution.py:73
  39.0 17.1 %reshape.203 = bf16[128,12,3584]{2,1,0:T(8,128)(2,1)} reshape(bf16[1536,3584]{1,0:T(8,128)(2,1)} %gather_fusion) | data formatting | bytes 22020096 | tf_op jit(solution)/shard_map/reshape | solution.py:73
  56.1 10.4 %all-to-all-start.1 = ((bf16[128,12,3584]{2,1,0:T(8,128)(2,1)}), bf16[128,12,3584]{2,1,0:T(8,128)(2,1)}, u32[]{:S(2)}, u32[]{:S(2)}) async-start(bf16[128,12,3584]{2,1,0:T(8,128)(2,1)} %reshape.203), calls=%async_computation.1 | async-start | bytes 29360128 | tf_op jit(solution)/shard_map/all_to_all | solution.py:75
  66.5 3.8 copy.41
  70.3 4.7 reshape_squeeze.3
  75.0 2.0 fusion.22
  76.9 1.8 copy.49
  78.8 1.6 copy.50
  80.4 0.2 convert_reduce_fusion
  80.7 185.7 %all-to-all-done.1 = bf16[128,12,3584]{2,1,0:T(8,128)(2,1)} async-done(((bf16[128,12,3584]{2,1,0:T(8,128)(2,1)}), bf16[128,12,3584]{2,1,0:T(8,128)(2,1)}, u32[]{:S(2)}, u32[]{:S(2)}) %all-to-all-start.1) | async-done | bytes 11010080 | tf_op jit(solution)/shard_map/all_to_all | solution.py:75
  266.5 17.2 %reshape.204 = bf16[1536,3584]{1,0:T(8,128)(2,1)} reshape(bf16[128,12,3584]{2,1,0:T(8,128)(2,1)} %all-to-all-done.1) | data formatting | bytes 22020096 | tf_op jit(solution)/shard_map/reshape | solution.py:85
  283.6 12.2 %multiply_reduce_fusion = (bf16[1536]{0:T(1024)(128)(2,1)S(1)}, bf16[1536,512]{0,1:T(8,128)(2,1)}, bf16[1536,512]{0,1:T(8,128)(2,1)}) fusion(bf16[1536,512]{0,1:T(8,128)(2,1)S(1)} %copy.49, bf16[1536,512]{0,1:T(8,128)(2,1)S(1)} %copy-done.2, f32[1536]{0:T(1024)S(1)} %reshape.208, bf16[1536,3584]{1,0:T(8,128)(2,1)} %reshape.204, bf16[1,512,3584]{2,1,0:T(8,128)(2,1)} %param.11), kind=kOutput, calls=%fused_computation.28 | convolution fusion | flops 5652085248 | bytes 20980736 | tf_op jit(solution)/shard_map/dot_general | solution.py:16
  295.8 0.8 convert_element_type.61
  296.6 15.8 %all-to-all-start.3 = ((bf16[128,1,12]{2,1,0:T(2,128)(2,1)}), bf16[128,1,12]{2,1,0:T(2,128)(2,1)S(1)}, u32[]{:S(2)}, u32[]{:S(2)}) async-start(bf16[128,1,12]{2,1,0:T(2,128)(2,1)} %convert_element_type.61), calls=%async_computation.3 | async-start | bytes 131072 | tf_op jit(solution)/shard_map/all_to_all | solution.py:95
  312.4 17.3 %convolution_convert_fusion = bf16[1536,3584]{1,0:T(8,128)(2,1)} fusion(bf16[1,3584,1024]{2,1,0:T(8,128)(2,1)} %param.10, bf16[1536,512]{0,1:T(8,128)(2,1)} %get-tuple-element.11, bf16[1536,512]{0,1:T(8,128)(2,1)} %get-tuple-element.10), kind=kOutput, calls=%fused_computation.5 | convolution fusion | flops 11286085632 | bytes 21495808 | tf_op jit(solution)/shard_map/dot_general | solution.py:25
  329.7 17.1 %reshape.205 = bf16[128,12,3584]{2,1,0:T(8,128)(2,1)} reshape(bf16[1536,3584]{1,0:T(8,128)(2,1)} %convolution_convert_fusion) | data formatting | bytes 22020096 | tf_op jit(solution)/shard_map/reshape | solution.py:89
  346.8 10.3 %all-to-all-start.2 = ((bf16[128,12,3584]{2,1,0:T(8,128)(2,1)}), bf16[128,12,3584]{2,1,0:T(8,128)(2,1)}, u32[]{:S(2)}, u32[]{:S(2)}) async-start(bf16[128,12,3584]{2,1,0:T(8,128)(2,1)} %reshape.205), calls=%async_computation.2 | async-start | bytes 29360128 | tf_op jit(solution)/shard_map/all_to_all | solution.py:88
  357.1 0.1 copy.47
  357.2 0.1 copy.46
  357.5 0.1 copy.44
  357.7 0.3 compare_select_fusion
  358.0 0.2 reshape.227
  358.2 11.7 %fusion.1 = bf16[1,512,3584]{2,1,0:T(8,128)(2,1)} fusion(bf16[1536,3584]{1,0:T(8,128)(2,1)} %reshape.204, bf16[1536,512]{0,1:T(8,128)(2,1)S(1)} %copy.49, f32[1536]{0:T(1024)S(1)} %reshape.208, bf16[1536,512]{0,1:T(8,128)(2,1)} %copy.50), kind=kOutput, calls=%fused_computation.9 | convolution fusion | flops 5646057472 | bytes 17831936 | tf_op jit(solution)/shard_map/dot_general | solution.py:29
  369.9 0.2 reduce.3
  370.1 0.1 reshape.207
  370.2 6.8 %gather_fusion.2 = bf16[1024]{0:T(1024)(128)(2,1)S(1)} fusion(bf16[1536]{0:T(1024)(128)(2,1)S(1)} %reshape.207, s32[1024]{0:T(1024)S(1)} %broadcast_clamp_fusion), kind=kCustom, calls=%fused_computation.2 | custom fusion | bytes 8192 | tf_op jit(solution)/shard_map/gather | solution.py:105
  377.0 0.2 reshape.252
  377.2 0.2 reduce_sum.52
  377.5 0.6 copy.48
  378.1 178.9 %all-to-all-done.2 = bf16[128,12,3584]{2,1,0:T(8,128)(2,1)} async-done(((bf16[128,12,3584]{2,1,0:T(8,128)(2,1)}), bf16[128,12,3584]{2,1,0:T(8,128)(2,1)}, u32[]{:S(2)}, u32[]{:S(2)}) %all-to-all-start.2) | async-done | bytes 11010080 | tf_op jit(solution)/shard_map/all_to_all | solution.py:88
  557.0 17.1 %reshape.206 = bf16[1536,3584]{1,0:T(8,128)(2,1)} reshape(bf16[128,12,3584]{2,1,0:T(8,128)(2,1)} %all-to-all-done.2) | data formatting | bytes 22020096 | tf_op jit(solution)/shard_map/reshape | solution.py:103
  574.1 19.3 %gather_fusion.1 = bf16[1024,3584]{1,0:T(8,128)(2,1)} fusion(bf16[1536,3584]{1,0:T(8,128)(2,1)} %reshape.206, s32[1024]{0:T(1024)S(1)} %broadcast_clamp_fusion.1), kind=kCustom, calls=%fused_computation.1 | custom fusion | bytes 14684160 | tf_op jit(solution)/shard_map/gather | solution.py:103
  593.4 8.9 %bitcast_reduce_fusion = bf16[128,3584]{1,0:T(8,128)(2,1)} fusion(bf16[1024,3584]{1,0:T(8,128)(2,1)} %gather_fusion.1), kind=kLoop, calls=%fused_computation.6 | loop fusion | flops 3211264 | bytes 8257536 | tf_op jit(solution)/shard_map/reduce_sum | solution.py:104
  (25 shorter events, 0.7 us)
Async XLA Ops:
  12.9 43.1 %all-to-all-start = ((bf16[128,1,12]{2,1,0:T(2,128)(2,1)}), bf16[128,1,12]{2,1,0:T(2,128)(2,1)S(1)}, u32[]{:S(2)}, u32[]{:S(2)}) async-start(bf16[128,1,12]{2,1,0:T(2,128)(2,1)} %all_to_all.21), calls=%async_computation | async-start | bytes 131072 | tf_op jit(solution)/shard_map/all_to_all | solution.py:76
  56.1 10.4 %copy-start.1 = (bf16[1,128,12,1024]{3,1,2,0:T(8,128)(2,1)S(1)}, bf16[1,128,12,1024]{3,1,2,0:T(8,128)(2,1)}, u32[]{:S(2)}) copy-start(bf16[1,128,12,1024]{3,1,2,0:T(8,128)(2,1)} %param.9) | copy-start | bytes 9437188
  56.1 210.4 %all-to-all-start.1 = ((bf16[128,12,3584]{2,1,0:T(8,128)(2,1)}), bf16[128,12,3584]{2,1,0:T(8,128)(2,1)}, u32[]{:S(2)}, u32[]{:S(2)}) async-start(bf16[128,12,3584]{2,1,0:T(8,128)(2,1)} %reshape.203), calls=%async_computation.1 | async-start | bytes 29360128 | tf_op jit(solution)/shard_map/all_to_all | solution.py:75
  76.9 1.9 copy-start
  80.7 202.9 %copy-start.2 = (bf16[1536,512]{0,1:T(8,128)(2,1)S(1)}, bf16[1536,512]{0,1:T(8,128)(2,1)}, u32[]{:S(2)}) copy-start(bf16[1536,512]{0,1:T(8,128)(2,1)} %copy.50) | copy-start | bytes 4718596
  296.6 50.2 %all-to-all-start.3 = ((bf16[128,1,12]{2,1,0:T(2,128)(2,1)}), bf16[128,1,12]{2,1,0:T(2,128)(2,1)S(1)}, u32[]{:S(2)}, u32[]{:S(2)}) async-start(bf16[128,1,12]{2,1,0:T(2,128)(2,1)} %convert_element_type.61), calls=%async_computation.3 | async-start | bytes 131072 | tf_op jit(solution)/shard_map/all_to_all | solution.py:95
  346.8 210.2 %all-to-all-start.2 = ((bf16[128,12,3584]{2,1,0:T(8,128)(2,1)}), bf16[128,12,3584]{2,1,0:T(8,128)(2,1)}, u32[]{:S(2)}, u32[]{:S(2)}) async-start(bf16[128,12,3584]{2,1,0:T(8,128)(2,1)} %reshape.205), calls=%async_computation.2 | async-start | bytes 29360128 | tf_op jit(solution)/shard_map/all_to_all | solution.py:88
where the time goes:
time: 614 us; the launch traced here: 602 us
  waiting for transfers between devices  365 us (59%)
  local copies, waits for them, and re-layouts  136 us (22%)
  starting transfers between devices  47.6 us (8%)
  matrix products  41.2 us (7%)
  other arithmetic  12.3 us (2%)
    all_to_all x1, waiting for transfers between devices, body(): lax.all_to_all(outgoing, ('node', 'local'), split_axis=0, concat_axis=0,...  186 us
    all_to_all x1, waiting for transfers between devices, body(): lax.all_to_all(x_part.reshape(unit_count, slot_cap, width), ('node', 'loc...  179 us
    gather x1, local copies, waits for them, and re-layouts, body(): picked = back_rows.reshape(-1, width)[slot_pos.reshape(tok_count, -1)]  19.3 us
    dot_general x1, matrix products, expert_backward(): lax.dot_general(d_pre, gate_up, (((1,), (1,)), ((), ())), preferred_eleme...  17.3 us
    reshape x1, local copies, waits for them, and re-layouts, body(): rows_in.reshape(-1, width)  17.2 us
    reshape x1, local copies, waits for them, and re-layouts, body(): picked = back_rows.reshape(-1, width)[slot_pos.reshape(tok_count, -1)]  17.1 us
    reshape x1, local copies, waits for them, and re-layouts, body(): outgoing = padded_rows[token_table].reshape(unit_count, slot_cap, width)  17.1 us
    reshape x1, local copies, waits for them, and re-layouts, body(): x_part.reshape(unit_count, slot_cap, width)  17.1 us
  transfers between devices with their start and end apart: 4, of which 2 were waited for; matrix products, arithmetic and copies ran while one was open for 17% of the time, Pallas kernels for 0%

commit v1 on v0

v1 whole, which is shorter than its diff:
```python
import functools

import jax
import jax.numpy as jnp
from jax import lax
from jax.experimental import pallas as pl
from jax.experimental.pallas import tpu as pltpu
from jax.sharding import PartitionSpec as P

NX = 4
PAD = 16
MESH = pl.DeviceIdType.MESH
F32 = jnp.float32
BF16 = jnp.bfloat16


def iota(shape, dim):
    return lax.broadcasted_iota(jnp.int32, shape, dim)


def mm(a, b):
    return jnp.dot(a, b, preferred_element_type=F32)


def mm_nt(a, b):
    return lax.dot_general(a, b, (((1,), (1,)), ((), ())), preferred_element_type=F32)


def kernel(
    B, C, SLOT,
    ids_ref, gates_ref, og_ref, saved_hbm, wgu_hbm, wd_hbm,
    ig_ref, gg_ref, dg_hbm,
    wgu, wd, send, recv, back, Y, GB, XP, RA, RB, GPS, GPR, S, wT, dtile, mt, dpre, dact,
    wsem, ssem, dsem, s1s, s1r, ags, agr, gbs, gbr, xps, rar, rbr, gps, gpr, rets, backr,
):
    T, D = og_ref.shape
    H = wd.shape[0]
    BLK = B * SLOT
    HALF = BLK // 2
    MSG = B * PAD
    ROWS = NX * BLK
    NSLOT = XP.shape[0]
    n = lax.axis_index("node")
    l = lax.axis_index("local")
    z, x = l // NX, l % NX
    right = (n, z * NX + (x + 1) % NX)
    left = (n, z * NX + (x + NX - 1) % NX)

    def peer(c, d):
        return ((n + d) % B, ((z + c) % C) * NX + x)

    def source(c, d):
        return ((n + B - d) % B, ((z + C - c) % C) * NX + x)

    def along(k):
        return (n, z * NX + (x + k) % NX)

    barrier = pltpu.get_barrier_semaphore()
    count = 0
    for c in range(C):
        for d in range(B):
            if c or d:
                pl.semaphore_signal(barrier, inc=1, device_id=peer(c, d), device_id_type=MESH)
                count += 1
    for k in range(1, NX):
        pl.semaphore_signal(barrier, inc=1, device_id=along(k), device_id_type=MESH)
        count += 1

    wd_copy = pltpu.make_async_copy(wd_hbm, wd, wsem.at[0])
    wgu_copy = pltpu.make_async_copy(wgu_hbm, wgu, wsem.at[1])

    def saved_start(c):
        slot = c % 2

        def one(i, _):
            j, d = i // B, i % B
            q = ((n + B - d) % B) * (C * NX) + ((z + C - c) % C) * NX + (x + j) % NX
            pltpu.make_async_copy(
                saved_hbm.at[q], S.at[slot, pl.ds(pl.multiple_of(i * PAD, PAD), PAD)], ssem.at[slot]
            ).start()
            return 0

        lax.fori_loop(0, NX * B, one, 0)

    def saved_wait(c):
        slot = c % 2
        pltpu.make_async_copy(S.at[slot], S.at[slot], ssem.at[slot]).wait()

    wd_copy.start()
    saved_start(0)
    wgu_copy.start()
    if C > 1:
        saved_start(1)

    lane = iota((T, 128), 1)

    def expert(k):
        return ids_ref[:, k : k + 1]

    hits = [lane == expert(k) for k in range(2)]
    per_token = hits[0].astype(F32) + hits[1].astype(F32)
    before = (iota((T, T), 1) < iota((T, T), 0)).astype(F32).astype(BF16)
    earlier = mm(before, per_token.astype(BF16))

    def rank(k):
        return jnp.sum(jnp.where(hits[k], earlier, 0.0), axis=1, keepdims=True).astype(jnp.int32)

    def block(k):
        e = expert(k)
        node = lax.shift_right_logical(e, jnp.int32(C.bit_length() - 1))
        zz = e & (C - 1)
        return ((zz - z + C) & (C - 1)) * B + ((node - n + B) & (B - 1))

    ranks = [rank(k) for k in range(2)]
    blocks = [block(k) for k in range(2)]
    slots = iota((T, C * MSG), 1)
    pick = jnp.zeros((T, C * MSG), F32)
    gate_rows = jnp.zeros((C * MSG, 128), F32)
    for k in range(2):
        pick += (slots == blocks[k] * PAD + ranks[k]).astype(F32)
        row_of = (slots == blocks[k] * PAD + SLOT).astype(F32)
        gate_at = jnp.where(lane == ranks[k], gates_ref[:, k : k + 1].astype(F32), 0.0)
        gate_rows += mm(jnp.transpose(row_of).astype(BF16), gate_at.astype(BF16))
    mt[...] = pick.astype(BF16)
    pick_t = jnp.transpose(pick).astype(BF16)
    TILE = 512 if D % 512 == 0 else D
    for i in range(D // TILE):
        cols = slice(i * TILE, (i + 1) * TILE)
        send[:, cols] = mm(pick_t, og_ref[:, cols]).astype(BF16)
    send[:, :128] = (send[:, :128].astype(F32) + gate_rows).astype(BF16)

    pl.semaphore_wait(barrier, count)

    for c in range(C):
        for d in range(B):
            rows = pl.ds((c * B + d) * PAD, PAD)
            if c or d:
                pltpu.make_async_remote_copy(
                    src_ref=send.at[rows], dst_ref=recv.at[rows], send_sem=s1s, recv_sem=s1r.at[c],
                    device_id=peer(c, d), device_id_type=MESH,
                ).start()
    recv[:PAD] = send[:PAD]

    i96, s128 = iota((BLK, MSG), 0), iota((BLK, MSG), 1)
    compact = (
        (i96 == SLOT * lax.shift_right_logical(s128, jnp.int32(4)) + (s128 & 15)) & ((s128 & 15) < SLOT)
    ).astype(F32).astype(BF16)
    s128b, i96b = iota((MSG, BLK), 0), iota((MSG, BLK), 1)
    expand = (
        (i96b == SLOT * lax.shift_right_logical(s128b, jnp.int32(4)) + (s128b & 15)) & ((s128b & 15) < SLOT)
    ).astype(F32).astype(BF16)
    gate_pick = (iota((PAD, MSG), 1) == iota((PAD, MSG), 0) * PAD + SLOT).astype(F32).astype(BF16)
    src_row, src_col = iota((BLK, PAD), 0), iota((BLK, PAD), 1)
    of_source = ((src_row >= SLOT * src_col) & (src_row < SLOT * src_col + SLOT)).astype(F32).astype(BF16)
    sc_row, sc_col = iota((PAD, BLK), 0), iota((PAD, BLK), 1)
    by_source = ((sc_col >= SLOT * sc_row) & (sc_col < SLOT * sc_row + SLOT)).astype(F32).astype(BF16)
    row_id = iota((BLK, 128), 0)
    src_id = jnp.zeros((BLK, 128), jnp.int32)
    for d in range(1, B):
        src_id += (row_id >= SLOT * d).astype(jnp.int32)
    slot_mask = iota((BLK, 128), 1) == row_id - SLOT * src_id

    def yrows(c, j, lo=0, size=None):
        return pl.ds(c * ROWS + j * BLK + lo, BLK if size is None else size)

    def remote(src, dst, ssem_, rsem_, dev):
        pltpu.make_async_remote_copy(
            src_ref=src, dst_ref=dst, send_sem=ssem_, recv_sem=rsem_, device_id=dev, device_id_type=MESH
        ).start()

    def wait_for(ref, sem):
        pltpu.make_async_copy(ref, ref, sem).wait()

    def gather_start(c):
        lo = PAD if c == 0 else 0
        if MSG > lo:
            wait_for(recv.at[pl.ds(c * MSG + lo, MSG - lo)], s1r.at[c])
        for i in range(D // TILE):
            cols = slice(i * TILE, (i + 1) * TILE)
            Y[yrows(c, 0), cols] = mm(compact, recv[c * MSG : (c + 1) * MSG, cols]).astype(BF16)
        GB[c, 0] = mm(gate_pick, recv[c * MSG : (c + 1) * MSG, :128]).astype(BF16)
        remote(Y.at[yrows(c, 0)], Y.at[yrows(c, 3)], ags, agr.at[c, 0], right)
        remote(Y.at[yrows(c, 0)], Y.at[yrows(c, 1)], ags, agr.at[c, 1], left)
        for k in range(1, NX):
            remote(GB.at[c, 0], GB.at[c, NX - k], gbs, gbr.at[c], along(k))

    def gather_forward(c):
        wait_for(Y.at[yrows(c, 3)], agr.at[c, 0])
        remote(Y.at[yrows(c, 3, 0, HALF)], Y.at[yrows(c, 2, 0, HALF)], ags, agr.at[c, 2], right)
        wait_for(Y.at[yrows(c, 1)], agr.at[c, 1])
        remote(Y.at[yrows(c, 1, HALF, HALF)], Y.at[yrows(c, 2, HALF, HALF)], ags, agr.at[c, 2], left)

    def compute(c):
        slot = c % 2
        xs = c % NSLOT
        wait_for(Y.at[yrows(c, 2)], agr.at[c, 2])
        wait_for(GB.at[c, pl.ds(1, NX - 1)], gbr.at[c])
        if c == 0:
            wd_copy.wait()
        NT = 256 if H % 256 == 0 else H
        for i in range(H // NT):
            dact[:, i * NT : (i + 1) * NT] = mm_nt(Y[c * ROWS : (c + 1) * ROWS, :], wd[i * NT : (i + 1) * NT, :])
        saved_wait(c)
        for j in range(NX):
            rows = slice(j * BLK, (j + 1) * BLK)
            pre = mm(compact, S[slot, j * MSG : (j + 1) * MSG, :])
            a, b = pre[:, :H], pre[:, H:]
            da = dact[rows, :]
            spread = mm(of_source, GB[c, j])
            scale = jnp.sum(jnp.where(slot_mask, spread, 0.0), axis=1, keepdims=True)
            s = jax.nn.sigmoid(a)
            act = a * s
            hidden = act * b
            part = jnp.sum(hidden * da, axis=1, keepdims=True)
            parts = jnp.where(slot_mask, part, 0.0).astype(BF16)
            GPS[c, j] = mm(by_source, parts).astype(BF16)
            dh = scale * da
            dpre[rows, :H] = (dh * b * s * (1.0 + a * (1.0 - s))).astype(BF16)
            dpre[rows, H:] = (dh * act).astype(BF16)
            dact[rows, :] = scale * hidden
        wT[:, c * ROWS : (c + 1) * ROWS] = jnp.transpose(dact[...]).astype(BF16)
        for k in range(1, NX):
            remote(GPS.at[c, k], GPR.at[c, NX - k], gps, gpr.at[c], along(k))
        if c + 2 < C:
            saved_start(c + 2)
        if c == 0:
            wgu_copy.wait()
        if c >= NSLOT:
            wait_for(XP.at[xs, pl.ds(BLK, ROWS - BLK)], xps.at[c - NSLOT])
        NU = 256 if D % 256 == 0 else D

        def tile(i, _):
            cols = pl.ds(pl.multiple_of(i * NU, NU), NU)
            XP[xs, :, cols] = mm_nt(dpre[...], wgu[cols, :]).astype(BF16)
            return 0

        lax.fori_loop(0, D // NU, tile, 0)

        def rows_of(j, lo, size):
            return pl.ds(j * BLK + lo, size)

        remote(XP.at[xs, rows_of(2, 0, HALF)], RA.at[c, 0], xps.at[c], rar.at[c, 0], right)
        remote(XP.at[xs, rows_of(2, HALF, HALF)], RA.at[c, 1], xps.at[c], rar.at[c, 1], left)
        remote(XP.at[xs, rows_of(1, HALF, HALF)], RB.at[c, 0, pl.ds(HALF, HALF)], xps.at[c], rbr.at[c, 0], right)
        remote(XP.at[xs, rows_of(3, 0, HALF)], RB.at[c, 1, pl.ds(0, HALF)], xps.at[c], rbr.at[c, 1], left)

    def reduce_middle(c):
        xs = c % NSLOT
        for side, j, lo, dev in ((0, 1, 0, right), (1, 3, HALF, left)):
            wait_for(RA.at[c, side], rar.at[c, side])
            rows = slice(j * BLK + lo, j * BLK + lo + HALF)
            XP[xs, rows, :] = (XP[xs, rows, :].astype(F32) + RA[c, side].astype(F32)).astype(BF16)
            remote(
                XP.at[xs, pl.ds(j * BLK + lo, HALF)], RB.at[c, side, pl.ds(lo, HALF)],
                xps.at[c], rbr.at[c, side], dev,
            )

    def reduce_end(c):
        xs = c % NSLOT
        wait_for(GPR.at[c, pl.ds(1, NX - 1)], gpr.at[c])
        total = GPS[c, 0].astype(F32)
        for k in range(1, NX):
            total += GPR[c, k].astype(F32)
        high = total.astype(BF16)
        low = (total - high.astype(F32)).astype(BF16)
        up = iota((MSG, PAD), 0) - iota((MSG, PAD), 1) * PAD
        gate_back = mm((up == SLOT).astype(F32).astype(BF16), high)
        gate_back += mm((up == SLOT + 1).astype(F32).astype(BF16), low)
        wait_for(RB.at[c, 0], rbr.at[c, 0])
        wait_for(RB.at[c, 1], rbr.at[c, 1])
        for i in range(D // TILE):
            cols = slice(i * TILE, (i + 1) * TILE)
            whole = XP[xs, :BLK, cols].astype(F32) + RB[c, 0, :, cols].astype(F32) + RB[c, 1, :, cols].astype(F32)
            out = mm(expand, whole.astype(BF16))
            if i == 0:
                recv[c * MSG : (c + 1) * MSG, :128] = (out[:, :128] + gate_back).astype(BF16)
                if TILE > 128:
                    recv[c * MSG : (c + 1) * MSG, 128:TILE] = out[:, 128:].astype(BF16)
            else:
                recv[c * MSG : (c + 1) * MSG, cols] = out.astype(BF16)
        for d in range(B):
            rows = pl.ds((c * B + d) * PAD, PAD)
            if c or d:
                remote(recv.at[rows], back.at[rows], rets, backr.at[c], source(c, d))
        if c == 0:
            back[:PAD] = recv[:PAD]

    NG = 256 if D % 256 == 0 else D
    tiles = D // NG

    def weight_grad():
        def out_copy(i, s):
            return pltpu.make_async_copy(
                dtile.at[s], dg_hbm.at[:, pl.ds(pl.multiple_of(i * NG, NG), NG)], dsem.at[s]
            )

        def tile(i, _):
            s = i % 2

            @pl.when(i >= 2)
            def _():
                out_copy(i - 2, s).wait()

            cols = pl.ds(pl.multiple_of(i * NG, NG), NG)
            dtile[s] = mm(wT[...], Y[:, cols]).astype(BF16)
            out_copy(i, s).start()
            return 0

        lax.fori_loop(0, tiles, tile, 0)
        for i in range(max(tiles - 2, 0), tiles):
            out_copy(i, i % 2).wait()

    gather_start(0)
    if C == 4:
        gather_start(1)
        gather_forward(0)
        gather_start(2)
        gather_forward(1)
        compute(0)
        gather_start(3)
        gather_forward(2)
        compute(1)
        reduce_middle(0)
        gather_forward(3)
        compute(2)
        reduce_end(0)
        reduce_middle(1)
        compute(3)
        reduce_end(1)
        reduce_middle(2)
        weight_grad()
        reduce_end(2)
        reduce_middle(3)
        reduce_end(3)
    else:
        for c in range(C):
            if c:
                gather_start(c)
            gather_forward(c)
            compute(c)
            reduce_middle(c)
            reduce_end(c)
        weight_grad()

    for c in range(C):
        lo = PAD if c == 0 else 0
        if MSG > lo:
            wait_for(back.at[pl.ds(c * MSG + lo, MSG - lo)], backr.at[c])
    for i in range(D // TILE):
        cols = slice(i * TILE, (i + 1) * TILE)
        ig_ref[:, cols] = mm(mt[...], back[:, cols]).astype(BF16)
    for k in range(2):
        at = slots - blocks[k] * PAD
        rows = ((at == SLOT) | (at == SLOT + 1)).astype(F32).astype(BF16)
        found = mm(rows, back[:, :128])
        gg_ref[:, k : k + 1] = jnp.sum(jnp.where(lane == ranks[k], found, 0.0), axis=1, keepdims=True)

    total = C * MSG - PAD
    wait_for(send.at[pl.ds(0, total)], s1s)
    wait_for(recv.at[pl.ds(0, total)], rets)
    wait_for(Y.at[pl.ds(0, C * 3 * BLK)], ags)
    for c in range(C):
        wait_for(GB.at[c, pl.ds(1, NX - 1)], gbs)
        wait_for(GPS.at[c, pl.ds(1, NX - 1)], gps)
    for c in range(max(0, C - NSLOT), C):
        wait_for(XP.at[c % NSLOT, pl.ds(BLK, ROWS - BLK)], xps.at[c])


def body(out_grad, gates, expert_ids, saved_pre, w_gate_up, w_down):
    T, D = out_grad.shape
    B = lax.axis_size("node")
    C = lax.axis_size("local") // NX
    Q, SLOT = saved_pre.shape[1:3]
    H = w_down.shape[1]
    saved = jnp.pad(saved_pre[0], ((0, 0), (0, PAD - SLOT), (0, 0)))
    BLK, MSG = B * SLOT, B * PAD
    ROWS = NX * BLK
    NSLOT = min(3, C)
    vm = pl.BlockSpec(memory_space=pltpu.VMEM)
    anywhere = pl.BlockSpec(memory_space=pl.ANY)
    dma = pltpu.SemaphoreType.DMA
    NG = 256 if D % 256 == 0 else D
    ig, gg, dg = pl.pallas_call(
        functools.partial(kernel, B, C, SLOT),
        out_shape=(
            jax.ShapeDtypeStruct((T, D), BF16),
            jax.ShapeDtypeStruct((T, 2), F32),
            jax.ShapeDtypeStruct((H, D), BF16),
        ),
        in_specs=[vm, vm, vm, anywhere, anywhere, anywhere],
        out_specs=(vm, vm, anywhere),
        scratch_shapes=[
            pltpu.VMEM((D, 2 * H), BF16),
            pltpu.VMEM((H, D), BF16),
            pltpu.VMEM((C * MSG, D), BF16),
            pltpu.VMEM((C * MSG, D), BF16),
            pltpu.VMEM((C * MSG, D), BF16),
            pltpu.VMEM((C * ROWS, D), BF16),
            pltpu.VMEM((C, NX, PAD, 128), BF16),
            pltpu.VMEM((NSLOT, ROWS, D), BF16),
            pltpu.VMEM((C, 2, BLK // 2, D), BF16),
            pltpu.VMEM((C, 2, BLK, D), BF16),
            pltpu.VMEM((C, NX, PAD, 128), BF16),
            pltpu.VMEM((C, NX, PAD, 128), BF16),
            pltpu.VMEM((2, NX * MSG, 2 * H), BF16),
            pltpu.VMEM((H, C * ROWS), BF16),
            pltpu.VMEM((2, H, NG), BF16),
            pltpu.VMEM((T, C * MSG), BF16),
            pltpu.VMEM((ROWS, 2 * H), BF16),
            pltpu.VMEM((ROWS, H), F32),
            dma((2,)),
            dma((2,)),
            dma((2,)),
            dma,
            dma((C,)),
            dma,
            dma((C, 3)),
            dma,
            dma((C,)),
            dma((C,)),
            dma((C, 2)),
            dma((C, 2)),
            dma,
            dma((C,)),
            dma,
            dma((C,)),
        ],
        compiler_params=pltpu.CompilerParams(
            collective_id=0, has_side_effects=True, vmem_limit_bytes=63 * 1024 * 1024
        ),
        cost_estimate=pl.CostEstimate(
            flops=2 * C * ROWS * D * 4 * H, bytes_accessed=25_000_000, transcendentals=C * ROWS * H
        ),
        name="moe_backward",
    )(expert_ids, gates, out_grad, saved, w_gate_up[0], w_down[0])
    return ig, gg, dg[None]


def solution(mesh):
    in_specs = (
        P(("node", "local"), None),
        P(("node", "local"), None),
        P(("node", "local"), None),
        P(("node", "local"), None, None, None),
        P(("node", "local"), None, None),
        P(("node", "local"), None, None),
    )
    out_specs = (
        P(("node", "local"), None),
        P(("node", "local"), None),
        P(("node", "local"), None, None),
    )
    return jax.shard_map(body, mesh=mesh, in_specs=in_specs, out_specs=out_specs, check_vma=False)
```

time: 614 us -> 257 us (0.42); the launches traced: 602 us -> 255 us
  waiting for transfers between devices: 365 us -> 0 us
  Pallas kernels: 0 us -> 238 us
  local copies, waits for them, and re-layouts: 136 us -> 17 us
  starting transfers between devices: 47.6 us -> 0 us
  matrix products: 41.2 us -> 0 us
  other arithmetic: 12.3 us -> 0 us
    all_to_all x4 -> x0, waiting for transfers between devices: 365 us -> none  [the longest x1 186 us: body(): lax.all_to_all(outgoing, ('node', 'local'), split_axis=0, concat_axis=0,...]
    pallas_call x0 -> x1, Pallas kernels: none -> 238 us  [body(): pl.pallas_call(functools.partial(kernel, B, C, SLOT), out_shape=(jax.Shap...]
    reshape x7 -> x0, local copies, waits for them, and re-layouts: 68.9 us -> none  [the longest x1 17.2 us: body(): rows_in.reshape(-1, width)]
    all_to_all x4 -> x0, starting transfers between devices: 47.6 us -> none  [the longest x1 15.8 us: body(): lax.all_to_all(gate_part.reshape(unit_count, slot_cap), ('node', 'local')...]
    dot_general x3 -> x0, matrix products: 41.2 us -> none  [the longest x1 17.3 us: expert_backward(): lax.dot_general(d_pre, gate_up, (((1,), (1,)), ((), ())), preferred_eleme...]
    gather x3 -> x0, local copies, waits for them, and re-layouts: 35.2 us -> none  [the longest x1 19.3 us: body(): picked = back_rows.reshape(-1, width)[slot_pos.reshape(tok_count, -1)]]
    scatter x2 -> x0, local copies, waits for them, and re-layouts: 11.9 us -> none  [the longest x1 7.59 us: body(): gate_slots = jnp.zeros((slot_total,), jnp.bfloat16).at[flat_pos].set(jnp....]
    reduce_sum x4 -> x0, other arithmetic: 10.5 us -> none  [the longest x1 8.93 us: body(): jnp.sum(picked.astype(jnp.float32), axis=1).astype(jnp.bfloat16)]
  transfers between devices with their start and end apart: 4 -> 0, of which waited for: 2 -> 0; matrix products, arithmetic and copies ran while one was open for 17% -> 0% of each run, Pallas kernels for 0% -> 0%
where the time goes in v1:
time: 257 us; the launch traced here: 255 us
  Pallas kernels  238 us (93%)
  local copies, waits for them, and re-layouts  17 us (7%)
    pallas_call x1, Pallas kernels, body(): pl.pallas_call(functools.partial(kernel, B, C, SLOT), out_shape=(jax.Shap...  238 us
    unnamed x6, local copies, waits for them, and re-layouts  14.2 us

profile of v1, /device:TPU:0, one launch (start us, length us, event | category | flops | bytes accessed | tf_op | source)
XLA Modules:
  0.0 255.4 jit_solution(10702125727788088152)
XLA Ops:
  0.6 1.4 copy.11.gates_ref
  2.0 1.4 copy.10.ids_ref
  3.4 3.7 %copy.14 = bf16[1,128,12,1024]{3,2,1,0:T(8,128)(2,1)S(1)} copy(bf16[1,128,12,1024]{3,1,2,0:T(8,128)(2,1)} %param.9) | data formatting | bytes 6291456 | tf_op args[3]
  7.1 2.8 %pad.4.saved_hbm = bf16[128,16,1024]{2,1,0:T(8,128)(2,1)} pad(bf16[128,12,1024]{2,1,0:T(8,128)(2,1)S(1)} %bitcast.6, bf16[]{:T(256)} %constant.2.clone.1), padding=0_0x0_4x0_0 | pad | bytes 7340034 | tf_op jit(solution)/shard_map/jit(_pad)/pad | solution.py:375
  9.9 237.7 %moe_backward.1 = (bf16[128,3584]{1,0:T(8,128)(2,1)}, f32[128,2]{1,0:T(8,128)}, bf16[512,3584]{1,0:T(8,128)(2,1)}) custom-call(s32[128,2]{1,0:T(8,128)} %copy.10.ids_ref, bf16[128,2]{1,0:T(8,128)(2,1)} %copy.11.gates_ref, bf16[128,3584]{1,0:T(8,128)(2,1)} %og_ref.1, bf16[128,16,1024]{2,1,0:T(8,128)(2,1)} %pad.4.saved_hbm, bf16[3584,1024]{1,0:T(8,128)(2,1)} %bitcast.8, ...), custom_call_target="tpu_custom_call" | custom-call | flops 22548578304 | bytes 25000000 | tf_op jit(solution)/shard_map/moe_backward/pallas_call | solution.py:383
  247.6 1.5 copy.12
  249.1 2.2 copy.17
  251.3 4.1 %copy.18 = bf16[1,512,3584]{2,1,0:T(8,128)(2,1)} copy(bf16[1,512,3584]{2,1,0:T(8,128)(2,1)} %bitcast.7) | data formatting | bytes 7340032

commit v2 on v1

v2 whole, which is shorter than its diff:
```python
import functools

import jax
import jax.numpy as jnp
from jax import lax
from jax.experimental import pallas as pl
from jax.experimental.pallas import tpu as pltpu
from jax.sharding import PartitionSpec as P

NX = 4
PAD = 16
TILE = 256
MESH = pl.DeviceIdType.MESH
F32 = jnp.float32
BF16 = jnp.bfloat16


def split(D):
    return max(TILE, 9 * D // 14 // TILE * TILE)


def iota(shape, dim):
    return lax.broadcasted_iota(jnp.int32, shape, dim)


def shr(v, bits):
    return lax.shift_right_logical(v, jnp.full(v.shape, bits, jnp.int32))


def log2(size):
    return size.bit_length() - 1


def mm(a, b):
    return jnp.dot(a, b, preferred_element_type=F32)


def mm_nt(a, b):
    return lax.dot_general(a, b, (((1,), (1,)), ((), ())), preferred_element_type=F32)


def hot(mask):
    return mask.astype(F32).astype(BF16)


def kernel(
    B, C, SLOT,
    ids_ref, gates_ref, og_ref, saved_hbm, wgu_hbm, wd_hbm,
    ig_ref, gg_ref, dg_hbm,
    wgu, wd, send, recv, back, Y, GB, XP, RA, RB, GPS, GPR, saved, dtile, mt, dpre, dact,
    IDS, TB, sendB, backB, RAB, RBB, selT, perm, permT,
    wsem, ssem, dsem, s1s, s1r, ags, agr, gbs, gbr, xps, rar, rbr, gps, gpr, rets, backr,
    idss, idsr, tbs, tbr, sbs, sbr, xpbs, bbr, pbs, rabr, rbbr,
):
    T, D = og_ref.shape
    H = wd.shape[0]
    DA = split(D)
    DB = D - DA
    BLK = B * SLOT
    HALF = BLK // 2
    MSG = B * PAD
    MB = NX * SLOT
    ROWS = NX * BLK
    NSLOT = XP.shape[0]
    LB, LC = log2(B), log2(C)
    colsA, colsB = pl.ds(0, DA), pl.ds(DA, DB)
    n = lax.axis_index("node")
    l = lax.axis_index("local")
    z, x = l // NX, l % NX
    right = (n, z * NX + (x + 1) % NX)
    left = (n, z * NX + (x + NX - 1) % NX)

    def peer(c, d):
        return ((n + d) % B, ((z + c) % C) * NX + x)

    def source(c, d):
        return ((n + B - d) % B, ((z + C - c) % C) * NX + x)

    def along(k):
        return (n, z * NX + (x + k) % NX)

    def remote(src, dst, ssem_, rsem_, dev):
        pltpu.make_async_remote_copy(
            src_ref=src, dst_ref=dst, send_sem=ssem_, recv_sem=rsem_, device_id=dev, device_id_type=MESH
        ).start()

    def wait_for(ref, sem):
        pltpu.make_async_copy(ref, ref, sem).wait()

    barrier = pltpu.get_barrier_semaphore()
    count = 0
    for k in range(1, NX):
        pl.semaphore_signal(barrier, inc=1, device_id=along(k), device_id_type=MESH)
        count += 1
    for c in range(C):
        for d in range(B):
            if c or d:
                pl.semaphore_signal(barrier, inc=1, device_id=peer(c, d), device_id_type=MESH)
                count += 1

    wd_copy = pltpu.make_async_copy(wd_hbm, wd, wsem.at[0])
    wgu_copy = pltpu.make_async_copy(wgu_hbm, wgu, wsem.at[1])

    Q = C * NX * B

    def staged(r):
        return NSLOT - 1, pl.ds(r // 2 % 2 * Q, Q), pl.ds(r % 2 * 2 * H, 2 * H)

    def stage(r):
        return pltpu.make_async_copy(saved_hbm.at[r], XP.at[staged(r)], ssem.at[r % 4])

    for r in range(4):
        stage(r).start()
    wd_copy.start()
    wgu_copy.start()

    IDS[0, :2] = ids_ref[...]
    TB[:T] = og_ref[:, DA:]
    NE = max(8, B * C)
    before = hot(iota((T, T), 0) < iota((T, T), 1))
    expert_row = iota((NE, T), 0)

    def route(ids):
        experts = [ids[k : k + 1] for k in range(2)]
        hits = [expert_row == e for e in experts]
        per_token = hits[0].astype(F32) + hits[1].astype(F32)
        earlier = mm(per_token.astype(BF16), before)
        out = []
        for k in range(2):
            rank = jnp.sum(jnp.where(hits[k], earlier, 0.0), axis=0, keepdims=True).astype(jnp.int32)
            zz = experts[k] & (C - 1)
            node = shr(experts[k], LC)
            blk = ((zz - z + C) & (C - 1)) * B + ((node - n + B) & (B - 1))
            out.append((blk, rank))
        return out

    own = route(ids_ref[...])
    slots = iota((C * MSG, T), 0)
    lane_slot = iota((128, T), 0)
    pick = jnp.zeros((C * MSG, T), F32)
    gate_rows = jnp.zeros((C * MSG, 128), F32)
    gates = gates_ref[...].astype(F32)
    for k, (blk, rank) in enumerate(own):
        pick += (slots == blk * PAD + rank).astype(F32)
        gate_at = jnp.where(lane_slot == rank, gates[k : k + 1], 0.0).astype(BF16)
        gate_rows += mm_nt(hot(slots == blk * PAD + SLOT), gate_at)
    mt[...] = jnp.transpose(pick).astype(BF16)
    pick = pick.astype(BF16)

    pl.semaphore_wait(barrier, count)

    for k in range(1, NX):
        remote(IDS.at[0], IDS.at[NX - k], idss, idsr, along(k))
    remote(TB.at[pl.ds(0, T)], TB.at[pl.ds(3 * T, T)], tbs, tbr.at[0], right)
    remote(TB.at[pl.ds(0, T)], TB.at[pl.ds(T, T)], tbs, tbr.at[1], left)

    for c in range(C):
        rows = slice(c * MSG, (c + 1) * MSG)
        for i in range(DA // TILE):
            cols = slice(i * TILE, (i + 1) * TILE)
            send[rows, cols] = mm(pick[rows], og_ref[:, cols]).astype(BF16)
        send[rows, :128] = (send[rows, :128].astype(F32) + gate_rows[rows]).astype(BF16)
        for d in range(B):
            at = pl.ds((c * B + d) * PAD, PAD)
            if c or d:
                remote(send.at[at, colsA], recv.at[at], s1s, s1r.at[c], peer(c, d))
    recv[:PAD] = send[:PAD, :DA]

    def row_parts(i):
        j = jnp.zeros(i.shape, jnp.int32)
        for k in range(1, NX):
            j += (i >= k * BLK).astype(jnp.int32)
        rest = i - j * BLK
        return j, shr(rest, LB), rest & (B - 1)

    _, r_i, d_i = row_parts(iota((BLK, MSG), 0))
    compact = hot(iota((BLK, MSG), 1) == d_i * PAD + r_i)
    _, r_l, d_l = row_parts(iota((MSG, BLK), 1))
    expand = hot(iota((MSG, BLK), 0) == d_l * PAD + r_l)
    gate_pick = hot(iota((PAD, MSG), 1) == iota((PAD, MSG), 0) * PAD + SLOT)
    of_source = hot((iota((BLK, PAD), 0) & (B - 1)) == iota((BLK, PAD), 1))
    by_source = hot((iota((PAD, BLK), 1) & (B - 1)) == iota((PAD, BLK), 0))
    slot_mask = iota((BLK, 128), 1) == shr(iota((BLK, 128), 0), LB)
    j_i, r_i, d_i = row_parts(iota((ROWS, ROWS), 0))
    perm[...] = hot(iota((ROWS, ROWS), 1) == d_i * MB + j_i * SLOT + r_i)
    j_l, r_l, d_l = row_parts(iota((ROWS, ROWS), 1))
    permT[...] = hot(iota((ROWS, ROWS), 0) == d_l * MB + j_l * SLOT + r_l)

    def sort_saved():
        row, col = iota((Q, Q), 0), iota((Q, Q), 1)
        cc, jj, dd = shr(row, LB + 2), shr(row, LB) & (NX - 1), row & (B - 1)
        q = ((n + B - dd) & (B - 1)) * (C * NX) + ((z + C - cc) & (C - 1)) * NX + ((x + jj) & (NX - 1))
        order = hot(col == q)
        for p in range(SLOT // 2):
            stage(2 * p).wait()
            stage(2 * p + 1).wait()
            pair = [mm(order, XP[staged(2 * p + h)]) for h in range(2)]
            for g in range(C * NX):
                both = jnp.concatenate([v[g * B : (g + 1) * B] for v in pair], axis=0)
                saved[g * BLK + 2 * B * p : g * BLK + 2 * B * (p + 1), :] = both.astype(BF16)
            if p + 2 < SLOT // 2:
                stage(2 * p + 4).start()
                stage(2 * p + 5).start()

    def b_forward():
        h = T // 2
        wait_for(TB.at[pl.ds(3 * T, T)], tbr.at[0])
        remote(TB.at[pl.ds(3 * T, h)], TB.at[pl.ds(2 * T, h)], tbs, tbr.at[2], right)
        wait_for(TB.at[pl.ds(T, T)], tbr.at[1])
        remote(TB.at[pl.ds(T + h, h)], TB.at[pl.ds(2 * T + h, h)], tbs, tbr.at[2], left)

    def b_routes():
        wait_for(IDS.at[pl.ds(1, NX - 1)], idsr)
        return [own] + [route(IDS[j, :2]) for j in range(1, NX)]

    def b_part(ref, c, lead):
        lo = MB if c == 0 else 0
        return ref.at[lead, pl.ds(lo, ROWS - lo)] if lead is not None else ref.at[pl.ds(lo, ROWS - lo)]

    def b_select(c, routes):
        slot = c % 2
        at = iota((ROWS, T), 0)
        parts = []
        for j in range(NX):
            part = jnp.zeros((ROWS, T), F32)
            for blk, rank in routes[j]:
                part += (at == (blk - c * B) * MB + j * SLOT + rank).astype(F32)
            parts.append(part)
            selT[j * T : (j + 1) * T, c * ROWS : (c + 1) * ROWS] = jnp.transpose(part).astype(BF16)
        sel = jnp.concatenate(parts, axis=1).astype(BF16)
        if c == 0:
            wait_for(TB.at[pl.ds(2 * T, T)], tbr.at[2])
        if c >= 2 and (B > 1 or c > 2):
            wait_for(b_part(sendB, c - 2, slot), sbs.at[slot])
        for i in range(DB // TILE):
            cols = slice(i * TILE, (i + 1) * TILE)
            sendB[slot, :, cols] = mm(sel, TB[:, cols]).astype(BF16)
        for d in range(B):
            if c or d:
                remote(
                    sendB.at[slot, pl.ds(d * MB, MB)], Y.at[pl.ds(c * ROWS + d * MB, MB), colsB],
                    sbs.at[slot], sbr.at[c], peer(c, d),
                )
            else:
                Y[:MB, DA:] = sendB[slot, :MB]

    def b_land(c):
        lo = MB if c == 0 else 0
        if ROWS > lo:
            wait_for(Y.at[pl.ds(c * ROWS + lo, ROWS - lo), colsB], sbr.at[c])
        rows = slice(c * ROWS, (c + 1) * ROWS)
        for i in range(DB // TILE):
            cols = slice(DA + i * TILE, DA + (i + 1) * TILE)
            Y[rows, cols] = mm(perm[...], Y[rows, cols]).astype(BF16)

    def yrows(c, j, lo=0, size=None):
        return pl.ds(c * ROWS + j * BLK + lo, BLK if size is None else size)

    def gather_start(c):
        lo = PAD if c == 0 else 0
        if MSG > lo:
            wait_for(recv.at[pl.ds(c * MSG + lo, MSG - lo)], s1r.at[c])
        own_rows = slice(c * ROWS, c * ROWS + BLK)
        for i in range(DA // TILE):
            cols = slice(i * TILE, (i + 1) * TILE)
            Y[own_rows, cols] = mm(compact, recv[c * MSG : (c + 1) * MSG, cols]).astype(BF16)
        GB[c, 0] = mm(gate_pick, recv[c * MSG : (c + 1) * MSG, :128]).astype(BF16)
        remote(Y.at[yrows(c, 0), colsA], Y.at[yrows(c, 3), colsA], ags, agr.at[c, 0], right)
        remote(Y.at[yrows(c, 0), colsA], Y.at[yrows(c, 1), colsA], ags, agr.at[c, 1], left)
        for k in range(1, NX):
            remote(GB.at[c, 0], GB.at[c, NX - k], gbs, gbr.at[c], along(k))

    def gather_forward(c):
        wait_for(Y.at[yrows(c, 3), colsA], agr.at[c, 0])
        remote(Y.at[yrows(c, 3, 0, HALF), colsA], Y.at[yrows(c, 2, 0, HALF), colsA], ags, agr.at[c, 2], right)
        wait_for(Y.at[yrows(c, 1), colsA], agr.at[c, 1])
        remote(Y.at[yrows(c, 1, HALF, HALF), colsA], Y.at[yrows(c, 2, HALF, HALF), colsA], ags, agr.at[c, 2], left)

    def compute(c):
        xs = c % NSLOT
        wait_for(Y.at[yrows(c, 2), colsA], agr.at[c, 2])
        wait_for(GB.at[c, pl.ds(1, NX - 1)], gbr.at[c])
        b_land(c)
        if c == 0:
            wd_copy.wait()
            wait_for(send.at[pl.ds(0, C * MSG - PAD), colsA], s1s)
        NT = min(TILE, H)
        for i in range(H // NT):
            dact[:, i * NT : (i + 1) * NT] = mm_nt(Y[c * ROWS : (c + 1) * ROWS, :], wd[i * NT : (i + 1) * NT, :])
        for j in range(NX):
            rows = slice(j * BLK, (j + 1) * BLK)
            at = c * ROWS + j * BLK
            a = saved[at : at + BLK, :H].astype(F32)
            b = saved[at : at + BLK, H:].astype(F32)
            da = dact[rows, :]
            spread = mm(of_source, GB[c, j])
            scale = jnp.sum(jnp.where(slot_mask, spread, 0.0), axis=1, keepdims=True)
            s = jax.nn.sigmoid(a)
            act = a * s
            hidden = act * b
            part = jnp.sum(hidden * da, axis=1, keepdims=True)
            parts = jnp.where(slot_mask, part, 0.0).astype(BF16)
            GPS[c, j] = mm(by_source, parts).astype(BF16)
            dh = scale * da
            dpre[rows, :H] = (dh * b * s * (1.0 + a * (1.0 - s))).astype(BF16)
            dpre[rows, H:] = (dh * act).astype(BF16)
            dact[rows, :] = scale * hidden
        for k in range(1, NX):
            remote(GPS.at[c, k], GPR.at[c, NX - k], gps, gpr.at[c], along(k))
        if c == 0:
            wgu_copy.wait()
        if c >= NSLOT:
            o = c - NSLOT
            wait_for(XP.at[xs, pl.ds(BLK, ROWS - BLK), colsA], xps.at[o])
            lo = MB if o == 0 else 0
            if ROWS > lo:
                wait_for(XP.at[xs, pl.ds(lo, ROWS - lo), colsB], xpbs.at[o])

        def tile_b(i, _):
            cols = pl.ds(pl.multiple_of(DA + i * TILE, TILE), TILE)
            XP[xs, :, cols] = mm(permT[...], mm_nt(dpre[...], wgu[cols, :]).astype(BF16)).astype(BF16)
            return 0

        lax.fori_loop(0, DB // TILE, tile_b, 0)
        for d in range(B):
            rows = pl.ds(d * MB, MB)
            if c or d:
                remote(
                    XP.at[xs, rows, colsB], backB.at[pl.ds((c * B + d) * MB, MB)],
                    xpbs.at[c], bbr.at[c], source(c, d),
                )
            else:
                backB[:MB] = XP[xs, :MB, DA:]

        def tile_a(i, _):
            cols = pl.ds(pl.multiple_of(i * TILE, TILE), TILE)
            XP[xs, :, cols] = mm_nt(dpre[...], wgu[cols, :]).astype(BF16)
            return 0

        lax.fori_loop(0, DA // TILE, tile_a, 0)

        def part_of(j, lo):
            return XP.at[xs, pl.ds(j * BLK + lo, HALF), colsA]

        remote(part_of(2, 0), RA.at[c, 0], xps.at[c], rar.at[c, 0], right)
        remote(part_of(2, HALF), RA.at[c, 1], xps.at[c], rar.at[c, 1], left)
        remote(part_of(1, HALF), RB.at[c, 0, pl.ds(HALF, HALF)], xps.at[c], rbr.at[c, 0], right)
        remote(part_of(3, 0), RB.at[c, 1, pl.ds(0, HALF)], xps.at[c], rbr.at[c, 1], left)
        send[:H, c * ROWS : (c + 1) * ROWS] = jnp.transpose(dact[...]).astype(BF16)

    def reduce_middle(c):
        xs = c % NSLOT
        for side, j, lo, dev in ((0, 1, 0, right), (1, 3, HALF, left)):
            wait_for(RA.at[c, side], rar.at[c, side])
            rows = slice(j * BLK + lo, j * BLK + lo + HALF)
            XP[xs, rows, :DA] = (XP[xs, rows, :DA].astype(F32) + RA[c, side].astype(F32)).astype(BF16)
            remote(
                XP.at[xs, pl.ds(j * BLK + lo, HALF), colsA], RB.at[c, side, pl.ds(lo, HALF)],
                xps.at[c], rbr.at[c, side], dev,
            )

    def reduce_end(c):
        xs = c % NSLOT
        wait_for(GPR.at[c, pl.ds(1, NX - 1)], gpr.at[c])
        total = GPS[c, 0].astype(F32)
        for k in range(1, NX):
            total += GPR[c, k].astype(F32)
        high = total.astype(BF16)
        low = (total - high.astype(F32)).astype(BF16)
        up = iota((MSG, PAD), 0) - iota((MSG, PAD), 1) * PAD
        gate_back = mm(hot(up == SLOT), high) + mm(hot(up == SLOT + 1), low)
        wait_for(RB.at[c, 0], rbr.at[c, 0])
        wait_for(RB.at[c, 1], rbr.at[c, 1])
        msg = slice(c * MSG, (c + 1) * MSG)
        for i in range(DA // TILE):
            cols = slice(i * TILE, (i + 1) * TILE)
            whole = XP[xs, :BLK, cols].astype(F32) + RB[c, 0, :, cols].astype(F32) + RB[c, 1, :, cols].astype(F32)
            out = mm(expand, whole.astype(BF16))
            if i == 0:
                recv[msg, :128] = (out[:, :128] + gate_back).astype(BF16)
                recv[msg, 128:TILE] = out[:, 128:].astype(BF16)
            else:
                recv[msg, cols] = out.astype(BF16)
        for d in range(B):
            rows = pl.ds((c * B + d) * PAD, PAD)
            if c or d:
                remote(recv.at[rows], back.at[rows], rets, backr.at[c], source(c, d))
        if c == 0:
            back[:PAD] = recv[:PAD]

    def b_sum():
        for c in range(C):
            lo = MB if c == 0 else 0
            if ROWS > lo:
                wait_for(backB.at[pl.ds(c * ROWS + lo, ROWS - lo)], bbr.at[c])
        wait_for(TB.at[pl.ds(0, 3 * T)], tbs)
        for i in range(DB // TILE):
            cols = slice(i * TILE, (i + 1) * TILE)
            TB[:, cols] = mm(selT[...], backB[:, cols]).astype(BF16)
        h = T // 2
        remote(TB.at[pl.ds(2 * T, h)], RAB.at[0], pbs, rabr.at[0], right)
        remote(TB.at[pl.ds(2 * T + h, h)], RAB.at[1], pbs, rabr.at[1], left)
        remote(TB.at[pl.ds(T + h, h)], RBB.at[0, pl.ds(h, h)], pbs, rbbr.at[0], right)
        remote(TB.at[pl.ds(3 * T, h)], RBB.at[1, pl.ds(0, h)], pbs, rbbr.at[1], left)

    def b_middle():
        h = T // 2
        for side, j, lo, dev in ((0, 1, 0, right), (1, 3, h, left)):
            wait_for(RAB.at[side], rabr.at[side])
            rows = slice(j * T + lo, j * T + lo + h)
            TB[rows, :] = (TB[rows, :].astype(F32) + RAB[side].astype(F32)).astype(BF16)
            remote(TB.at[pl.ds(j * T + lo, h)], RBB.at[side, pl.ds(lo, h)], pbs, rbbr.at[side], dev)

    def b_end():
        wait_for(RBB.at[0], rbbr.at[0])
        wait_for(RBB.at[1], rbbr.at[1])
        ig_ref[:, DA:] = (TB[:T].astype(F32) + RBB[0].astype(F32) + RBB[1].astype(F32)).astype(BF16)

    tiles = D // TILE

    def weight_grad(first, last):
        def out_copy(i, s):
            return pltpu.make_async_copy(
                dtile.at[s], dg_hbm.at[:, pl.ds(pl.multiple_of(i * TILE, TILE), TILE)], dsem.at[s]
            )

        def tile(i, _):
            s = i % 2

            @pl.when(i >= first + 2)
            def _():
                out_copy(i - 2, s).wait()

            cols = pl.ds(pl.multiple_of(i * TILE, TILE), TILE)
            dtile[s] = mm(send[:H, : C * ROWS], Y[:, cols]).astype(BF16)
            out_copy(i, s).start()
            return 0

        lax.fori_loop(first, last, tile, 0)
        for i in range(max(last - 2, first), last):
            out_copy(i, i % 2).wait()

    if C == 4:
        b_forward()
        gather_start(0)
        routes = b_routes()
        b_select(0, routes)
        gather_start(1)
        b_select(1, routes)
        gather_forward(0)
        sort_saved()
        gather_start(2)
        gather_forward(1)
        b_select(2, routes)
        gather_start(3)
        b_select(3, routes)
        compute(0)
        gather_forward(2)
        compute(1)
        gather_forward(3)
        reduce_middle(0)
        compute(2)
        reduce_end(0)
        reduce_middle(1)
        compute(3)
        reduce_end(1)
        reduce_middle(2)
        weight_grad(0, tiles // 2)
        b_sum()
        reduce_end(2)
        reduce_middle(3)
        b_middle()
        weight_grad(tiles // 2, tiles)
        reduce_end(3)
        b_end()
    else:
        b_forward()
        sort_saved()
        routes = b_routes()
        for c in range(C):
            b_select(c, routes)
            gather_start(c)
            gather_forward(c)
            compute(c)
            reduce_middle(c)
            reduce_end(c)
        b_sum()
        b_middle()
        b_end()
        weight_grad(0, tiles)

    for c in range(C):
        lo = PAD if c == 0 else 0
        if MSG > lo:
            wait_for(back.at[pl.ds(c * MSG + lo, MSG - lo)], backr.at[c])
    for i in range(DA // TILE):
        cols = slice(i * TILE, (i + 1) * TILE)
        ig_ref[:, cols] = mm(mt[...], back[:, cols]).astype(BF16)
    back_gates = jnp.transpose(back[:, :128].astype(F32)).astype(BF16)
    for k, (blk, rank) in enumerate(own):
        at = slots - blk * PAD
        found = mm(back_gates, hot((at == SLOT) | (at == SLOT + 1)))
        gg_ref[k : k + 1, :] = jnp.sum(jnp.where(lane_slot == rank, found, 0.0), axis=0, keepdims=True)

    wait_for(recv.at[pl.ds(0, C * MSG - PAD)], rets)
    wait_for(Y.at[pl.ds(0, C * 3 * BLK), colsA], ags)
    wait_for(IDS.at[pl.ds(1, NX - 1)], idss)
    wait_for(TB.at[pl.ds(0, 3 * T)], pbs)
    for c in range(C):
        wait_for(GB.at[c, pl.ds(1, NX - 1)], gbs)
        wait_for(GPS.at[c, pl.ds(1, NX - 1)], gps)
    for c in range(max(0, C - 2), C):
        lo = MB if c == 0 else 0
        if ROWS > lo:
            wait_for(sendB.at[c % 2, pl.ds(lo, ROWS - lo)], sbs.at[c % 2])
    for c in range(max(0, C - NSLOT), C):
        lo = MB if c == 0 else 0
        wait_for(XP.at[c % NSLOT, pl.ds(BLK, ROWS - BLK), colsA], xps.at[c])
        if ROWS > lo:
            wait_for(XP.at[c % NSLOT, pl.ds(lo, ROWS - lo), colsB], xpbs.at[c])


def body(out_grad, gates, expert_ids, saved_pre, w_gate_up, w_down):
    T, D = out_grad.shape
    B = lax.axis_size("node")
    C = lax.axis_size("local") // NX
    Q, SLOT = saved_pre.shape[1:3]
    H = w_down.shape[1]
    DA = split(D)
    DB = D - DA
    saved = jnp.transpose(saved_pre[0], (1, 0, 2))
    BLK, MSG = B * SLOT, B * PAD
    ROWS = NX * BLK
    NSLOT = min(3, C)
    vm = pl.BlockSpec(memory_space=pltpu.VMEM)
    anywhere = pl.BlockSpec(memory_space=pl.ANY)
    dma = pltpu.SemaphoreType.DMA
    ig, gg, dg = pl.pallas_call(
        functools.partial(kernel, B, C, SLOT),
        out_shape=(
            jax.ShapeDtypeStruct((T, D), BF16),
            jax.ShapeDtypeStruct((2, T), F32),
            jax.ShapeDtypeStruct((H, D), BF16),
        ),
        in_specs=[vm, vm, vm, anywhere, anywhere, anywhere],
        out_specs=(vm, vm, anywhere),
        scratch_shapes=[
            pltpu.VMEM((D, 2 * H), BF16),
            pltpu.VMEM((H, D), BF16),
            pltpu.VMEM((max(C * MSG, H), max(DA, C * ROWS)), BF16),
            pltpu.VMEM((C * MSG, DA), BF16),
            pltpu.VMEM((C * MSG, DA), BF16),
            pltpu.VMEM((C * ROWS, D), BF16),
            pltpu.VMEM((C, NX, PAD, 128), BF16),
            pltpu.VMEM((NSLOT, ROWS, D), BF16),
            pltpu.VMEM((C, 2, BLK // 2, DA), BF16),
            pltpu.VMEM((C, 2, BLK, DA), BF16),
            pltpu.VMEM((C, NX, PAD, 128), BF16),
            pltpu.VMEM((C, NX, PAD, 128), BF16),
            pltpu.VMEM((C * ROWS, 2 * H), BF16),
            pltpu.VMEM((2, H, TILE), BF16),
            pltpu.VMEM((T, C * MSG), BF16),
            pltpu.VMEM((ROWS, 2 * H), BF16),
            pltpu.VMEM((ROWS, H), F32),
            pltpu.VMEM((NX, 8, T), jnp.int32),
            pltpu.VMEM((NX * T, DB), BF16),
            pltpu.VMEM((2, ROWS, DB), BF16),
            pltpu.VMEM((C * ROWS, DB), BF16),
            pltpu.VMEM((2, T // 2, DB), BF16),
            pltpu.VMEM((2, T, DB), BF16),
            pltpu.VMEM((NX * T, C * ROWS), BF16),
            pltpu.VMEM((ROWS, ROWS), BF16),
            pltpu.VMEM((ROWS, ROWS), BF16),
            dma((2,)),
            dma((4,)),
            dma((2,)),
            dma,
            dma((C,)),
            dma,
            dma((C, 3)),
            dma,
            dma((C,)),
            dma((C,)),
            dma((C, 2)),
            dma((C, 2)),
            dma,
            dma((C,)),
            dma,
            dma((C,)),
            dma,
            dma,
            dma,
            dma((3,)),
            dma((2,)),
            dma((C,)),
            dma((C,)),
            dma((C,)),
            dma,
            dma((2,)),
            dma((2,)),
        ],
        compiler_params=pltpu.CompilerParams(
            collective_id=0, has_side_effects=True, vmem_limit_bytes=63 * 1024 * 1024
        ),
        cost_estimate=pl.CostEstimate(
            flops=2 * C * ROWS * D * 4 * H, bytes_accessed=25_000_000, transcendentals=C * ROWS * H
        ),
        name="moe_backward",
    )(expert_ids.T, gates.T, out_grad, saved, w_gate_up[0], w_down[0])
    return ig, gg.T, dg[None]


def solution(mesh):
    in_specs = (
        P(("node", "local"), None),
        P(("node", "local"), None),
        P(("node", "local"), None),
        P(("node", "local"), None, None, None),
        P(("node", "local"), None, None),
        P(("node", "local"), None, None),
    )
    out_specs = (
        P(("node", "local"), None),
        P(("node", "local"), None),
        P(("node", "local"), None, None),
    )
    return jax.shard_map(body, mesh=mesh, in_specs=in_specs, out_specs=out_specs, check_vma=False)
```

time: 257 us -> 205 us (0.80)
  the two profiles are of different devices: /device:TPU:0 before, /device:TPU:58 now
where the time goes in v2:
time: 205 us; the launch traced here: 204 us
  Pallas kernels  196 us (96%)
  local copies, waits for them, and re-layouts  7.49 us (4%)
    pallas_call x1, Pallas kernels, body(): pl.pallas_call(functools.partial(kernel, B, C, SLOT), out_shape=(jax.Shap...  196 us
    unnamed x3, local copies, waits for them, and re-layouts  7.49 us

profile of v2, /device:TPU:58, one launch (start us, length us, event | category | flops | bytes accessed | tf_op | source)
XLA Modules:
  0.0 204.3 jit_solution(9771101387471373458)
XLA Ops:
  0.6 196.2 %moe_backward.1 = (bf16[128,3584]{1,0:T(8,128)(2,1)}, f32[2,128]{1,0:T(2,128)}, bf16[512,3584]{1,0:T(8,128)(2,1)}) custom-call(s32[2,128]{1,0:T(2,128)} %bitcast.14, bf16[2,128]{1,0:T(2,128)(2,1)} %bitcast.15, bf16[128,3584]{1,0:T(8,128)(2,1)} %og_ref.1, bf16[12,128,1024]{2,1,0:T(8,128)(2,1)} %bitcast.13, bf16[3584,1024]{1,0:T(8,128)(2,1)} %bitcast.11, ...), custom_call_target="tpu_custom_call" | custom-call | flops 22548578304 | bytes 25000000 | tf_op jit(solution)/shard_map/moe_backward/pallas_call | solution.py:538
  196.8 2.2 %copy.12 = bf16[128,3584]{1,0:T(8,128)(2,1)} copy(bf16[128,3584]{1,0:T(8,128)(2,1)} %get-tuple-element.12) | data formatting | bytes 1835008
  199.0 1.2 copy.13
  200.2 4.1 %copy.14 = bf16[1,512,3584]{2,1,0:T(8,128)(2,1)} copy(bf16[1,512,3584]{2,1,0:T(8,128)(2,1)} %bitcast.9) | data formatting | bytes 7340032

commit v3 on v2

--- a/solution.py
+++ b/solution.py
@@ -16,7 +16,7 @@
 
 
 def split(D):
-    return max(TILE, 9 * D // 14 // TILE * TILE)
+    return max(TILE, 11 * D // 14 // TILE * TILE)
 
 
 def iota(shape, dim):
@@ -70,11 +70,22 @@
     right = (n, z * NX + (x + 1) % NX)
     left = (n, z * NX + (x + NX - 1) % NX)
 
+    CORES = 2 if B > C else 1
+    YS = B // CORES
+    y, core = n // CORES, n % CORES
+    LCO = log2(CORES)
+    even = YS == C
+
+    def offsets(c, d):
+        return (d % C, (c + C - d % C) % C, d // C) if even else (c, d // CORES, d % CORES)
+
     def peer(c, d):
-        return ((n + d) % B, ((z + c) % C) * NX + x)
+        dz, dy, dc = offsets(c, d)
+        return (((y + dy) % YS) * CORES + (core + dc) % CORES, ((z + dz) % C) * NX + x)
 
     def source(c, d):
-        return ((n + B - d) % B, ((z + C - c) % C) * NX + x)
+        dz, dy, dc = offsets(c, d)
+        return (((y + YS - dy) % YS) * CORES + (core + CORES - dc) % CORES, ((z + C - dz) % C) * NX + x)
 
     def along(k):
         return (n, z * NX + (x + k) % NX)
@@ -130,7 +141,10 @@
             rank = jnp.sum(jnp.where(hits[k], earlier, 0.0), axis=0, keepdims=True).astype(jnp.int32)
             zz = experts[k] & (C - 1)
             node = shr(experts[k], LC)
-            blk = ((zz - z + C) & (C - 1)) * B + ((node - n + B) & (B - 1))
+            dz = (zz - z + C) & (C - 1)
+            dy = (shr(node, LCO) - y + YS) & (YS - 1)
+            dc = (node - core + CORES) & (CORES - 1)
+            blk = ((dy + dz) & (C - 1)) * B + dc * C + dz if even else dz * B + dy * CORES + dc
             out.append((blk, rank))
         return out
 
@@ -189,7 +203,13 @@
     def sort_saved():
         row, col = iota((Q, Q), 0), iota((Q, Q), 1)
         cc, jj, dd = shr(row, LB + 2), shr(row, LB) & (NX - 1), row & (B - 1)
-        q = ((n + B - dd) & (B - 1)) * (C * NX) + ((z + C - cc) & (C - 1)) * NX + ((x + jj) & (NX - 1))
+        if even:
+            dz, dc = dd & (C - 1), shr(dd, LC)
+            dy = (cc + C - dz) & (C - 1)
+        else:
+            dz, dy, dc = cc, shr(dd, LCO), dd & (CORES - 1)
+        node = ((y + YS - dy) & (YS - 1)) * CORES + ((core + CORES - dc) & (CORES - 1))
+        q = node * (C * NX) + ((z + C - dz) & (C - 1)) * NX + ((x + jj) & (NX - 1))
         order = hot(col == q)
         for p in range(SLOT // 2):
             stage(2 * p).wait()

time: 205 us -> 194 us (0.946)
  the two profiles are of different devices: /device:TPU:58 before, /device:TPU:0 now
where the time goes in v3:
time: 194 us; the launch traced here: 191 us
  Pallas kernels  183 us (94%)
  local copies, waits for them, and re-layouts  7.49 us (4%)
    pallas_call x1, Pallas kernels, body(): pl.pallas_call(functools.partial(kernel, B, C, SLOT), out_shape=(jax.Shap...  183 us
    unnamed x3, local copies, waits for them, and re-layouts  7.49 us

profile of v3, /device:TPU:0, one launch (start us, length us, event | category | flops | bytes accessed | tf_op | source)
XLA Modules:
  0.0 191.4 jit_solution(16820461165750287338)
XLA Ops:
  0.6 183.3 %moe_backward.1 = (bf16[128,3584]{1,0:T(8,128)(2,1)}, f32[2,128]{1,0:T(2,128)}, bf16[512,3584]{1,0:T(8,128)(2,1)}) custom-call(s32[2,128]{1,0:T(2,128)} %bitcast.14, bf16[2,128]{1,0:T(2,128)(2,1)} %bitcast.15, bf16[128,3584]{1,0:T(8,128)(2,1)} %og_ref.1, bf16[12,128,1024]{2,1,0:T(8,128)(2,1)} %bitcast.13, bf16[3584,1024]{1,0:T(8,128)(2,1)} %bitcast.11, ...), custom_call_target="tpu_custom_call" | custom-call | flops 22548578304 | bytes 25000000 | tf_op jit(solution)/shard_map/moe_backward/pallas_call | solution.py:558
  183.9 2.2 %copy.12 = bf16[128,3584]{1,0:T(8,128)(2,1)} copy(bf16[128,3584]{1,0:T(8,128)(2,1)} %get-tuple-element.12) | data formatting | bytes 1835008
  186.1 1.2 copy.13
  187.3 4.1 %copy.14 = bf16[1,512,3584]{2,1,0:T(8,128)(2,1)} copy(bf16[1,512,3584]{2,1,0:T(8,128)(2,1)} %bitcast.9) | data formatting | bytes 7340032

commit v4 on v3

v4 whole, which is shorter than its diff:
```python
import functools

import jax
import jax.numpy as jnp
from jax import lax
from jax.experimental import pallas as pl
from jax.experimental.pallas import tpu as pltpu
from jax.sharding import PartitionSpec as P

NX = 4
PAD = 16
TILE = 256
MESH = pl.DeviceIdType.MESH
F32 = jnp.float32
BF16 = jnp.bfloat16


def split(D):
    return max(TILE, 11 * D // 14 // TILE * TILE)


def iota(shape, dim):
    return lax.broadcasted_iota(jnp.int32, shape, dim)


def shr(v, bits):
    return lax.shift_right_logical(v, jnp.full(v.shape, bits, jnp.int32))


def log2(size):
    return size.bit_length() - 1


def mm(a, b):
    return jnp.dot(a, b, preferred_element_type=F32)


def mm_nt(a, b):
    return lax.dot_general(a, b, (((1,), (1,)), ((), ())), preferred_element_type=F32)


def hot(mask):
    return mask.astype(F32).astype(BF16)


def plan(B, C):
    cores = 2 if B > C else 1
    even = B // cores == C
    chunks = C * cores if even else C
    return cores, chunks, B * C // chunks, even


def kernel(
    B, C, SLOT, NSLOT,
    ids_ref, gates_ref, og_hbm, saved_hbm, wgu_hbm, wd_hbm,
    ig_ref, gg_ref, dg_ref,
    og_ref, wgu, send, recv, back, Y, GB, XP, RA, RB, GPS, GPR, saved, mt, dpre, dact,
    IDS, TB, sendB, backB, RAB, RBB, selT, perm, permT,
    wsem, ssem, s1s, s1r, ags, agr, gbs, gbr, xps, rar, rbr, gps, gpr, rets, backr,
    idss, idsr, tbs, tbr, sbs, sbr, xpbs, bbr, pbs, rabr, rbbr,
):
    T, D = og_ref.shape
    H = dg_ref.shape[0]
    wd = dg_ref
    DA = split(D)
    DB = D - DA
    CORES, K, G, even = plan(B, C)
    BLK = G * SLOT
    MSG = G * PAD
    MB = NX * SLOT
    ROWS = NX * BLK
    NSB = sendB.shape[0]
    LG, LC = log2(G), log2(C)
    colsA, colsB = pl.ds(0, DA), pl.ds(DA, DB)
    n = lax.axis_index("node")
    l = lax.axis_index("local")
    z, x = l // NX, l % NX
    right = (n, z * NX + (x + 1) % NX)
    left = (n, z * NX + (x + NX - 1) % NX)

    YS = B // CORES
    y, core = n // CORES, n % CORES
    LCO = log2(CORES)

    def offsets(c, d):
        return (d, (c // CORES + C - d) % C, c % CORES) if even else (c, d // CORES, d % CORES)

    def peer(c, d):
        dz, dy, dc = offsets(c, d)
        return (((y + dy) % YS) * CORES + (core + dc) % CORES, ((z + dz) % C) * NX + x)

    def source(c, d):
        dz, dy, dc = offsets(c, d)
        return (((y + YS - dy) % YS) * CORES + (core + CORES - dc) % CORES, ((z + C - dz) % C) * NX + x)

    def along(k):
        return (n, z * NX + (x + k) % NX)

    def remote(src, dst, ssem_, rsem_, dev):
        pltpu.make_async_remote_copy(
            src_ref=src, dst_ref=dst, send_sem=ssem_, recv_sem=rsem_, device_id=dev, device_id_type=MESH
        ).start()

    def wait_for(ref, sem):
        pltpu.make_async_copy(ref, ref, sem).wait()

    barrier = pltpu.get_barrier_semaphore()
    count = 0
    for k in range(1, NX):
        pl.semaphore_signal(barrier, inc=1, device_id=along(k), device_id_type=MESH)
        count += 1
    for c in range(K):
        for d in range(G):
            if c or d:
                pl.semaphore_signal(barrier, inc=1, device_id=peer(c, d), device_id_type=MESH)
                count += 1

    wd_copy = pltpu.make_async_copy(wd_hbm, wd, wsem.at[0])
    wgu_copy = pltpu.make_async_copy(wgu_hbm, wgu, wsem.at[1])

    Q = C * NX * B
    QUADS = SLOT // 4
    first_row = NSLOT * ROWS - 4 * Q

    def stage(r):
        dst = XP.at[pl.ds(first_row + r % 4 * Q, Q), pl.ds(r // 4 * 2 * H, 2 * H)]
        return pltpu.make_async_copy(saved_hbm.at[r], dst, ssem)

    og_copy = pltpu.make_async_copy(og_hbm, og_ref, wsem.at[2])
    og_copy.start()
    for r in range(SLOT):
        stage(r).start()
    wd_copy.start()
    wgu_copy.start()

    IDS[0, :2] = ids_ref[...]
    NE = max(8, B * C)
    before = hot(iota((T, T), 0) < iota((T, T), 1))
    expert_row = iota((NE, T), 0)

    def route(ids):
        experts = [ids[k : k + 1] for k in range(2)]
        hits = [expert_row == e for e in experts]
        per_token = hits[0].astype(F32) + hits[1].astype(F32)
        earlier = mm(per_token.astype(BF16), before)
        out = []
        for k in range(2):
            rank = jnp.sum(jnp.where(hits[k], earlier, 0.0), axis=0, keepdims=True).astype(jnp.int32)
            zz = experts[k] & (C - 1)
            node = shr(experts[k], LC)
            dz = (zz - z + C) & (C - 1)
            dy = (shr(node, LCO) - y + YS) & (YS - 1)
            dc = (node - core + CORES) & (CORES - 1)
            blk = (((dy + dz) & (C - 1)) * CORES + dc) * G + dz if even else dz * G + dy * CORES + dc
            out.append((blk, rank))
        return out

    own = route(ids_ref[...])
    slots = iota((K * MSG, T), 0)
    lane_slot = iota((128, T), 0)
    pick = jnp.zeros((K * MSG, T), F32)
    gate_rows = jnp.zeros((K * MSG, 128), F32)
    gates = gates_ref[...].astype(F32)
    for k, (blk, rank) in enumerate(own):
        pick += (slots == blk * PAD + rank).astype(F32)
        gate_at = jnp.where(lane_slot == rank, gates[k : k + 1], 0.0).astype(BF16)
        gate_rows += mm_nt(hot(slots == blk * PAD + SLOT), gate_at)
    mt[...] = jnp.transpose(pick).astype(BF16)
    pick = pick.astype(BF16)
    og_copy.wait()
    TB[:T] = og_ref[:, DA:]

    pl.semaphore_wait(barrier, count)

    for k in range(1, NX):
        remote(IDS.at[0], IDS.at[NX - k], idss, idsr, along(k))
    remote(TB.at[pl.ds(0, T)], TB.at[pl.ds(3 * T, T)], tbs, tbr.at[0], right)
    remote(TB.at[pl.ds(0, T)], TB.at[pl.ds(T, T)], tbs, tbr.at[1], left)

    HEAD = K // 4 if K >= 4 else K
    for g in range(0, K, HEAD):
        rows = slice(g * MSG, (g + HEAD) * MSG)
        for i in range(DA // TILE):
            cols = slice(i * TILE, (i + 1) * TILE)
            send[rows, cols] = mm(pick[rows], og_ref[:, cols]).astype(BF16)
        send[rows, :128] = (send[rows, :128].astype(F32) + gate_rows[rows]).astype(BF16)
        for c in range(g, g + HEAD):
            for d in range(G):
                at = pl.ds((c * G + d) * PAD, PAD)
                if c or d:
                    remote(send.at[at, colsA], recv.at[at], s1s, s1r.at[c], peer(c, d))
    recv[:PAD] = send[:PAD, :DA]

    def row_parts(i):
        j = jnp.zeros(i.shape, jnp.int32)
        for k in range(1, NX):
            j += (i >= k * BLK).astype(jnp.int32)
        rest = i - j * BLK
        return j, shr(rest, LG), rest & (G - 1)

    _, r_i, d_i = row_parts(iota((BLK, MSG), 0))
    compact = hot(iota((BLK, MSG), 1) == d_i * PAD + r_i)
    _, r_l, d_l = row_parts(iota((MSG, BLK), 1))
    expand = hot(iota((MSG, BLK), 0) == d_l * PAD + r_l)
    gate_pick = hot(iota((PAD, MSG), 1) == iota((PAD, MSG), 0) * PAD + SLOT)
    of_source = hot((iota((BLK, PAD), 0) & (G - 1)) == iota((BLK, PAD), 1))
    by_source = hot((iota((PAD, BLK), 1) & (G - 1)) == iota((PAD, BLK), 0))
    slot_mask = iota((BLK, 128), 1) == shr(iota((BLK, 128), 0), LG)
    j_i, r_i, d_i = row_parts(iota((ROWS, ROWS), 0))
    perm[...] = hot(iota((ROWS, ROWS), 1) == d_i * MB + j_i * SLOT + r_i)
    j_l, r_l, d_l = row_parts(iota((ROWS, ROWS), 1))
    permT[...] = hot(iota((ROWS, ROWS), 0) == d_l * MB + j_l * SLOT + r_l)

    def sort_saved():
        row, col = iota((K * NX * 4 * G, 4 * Q), 0), iota((K * NX * 4 * G, 4 * Q), 1)
        r, d, j, c = shr(row, LG) & 3, row & (G - 1), shr(row, LG + 2) & (NX - 1), shr(row, LG + 4)
        if even:
            dz, dc = d, c & (CORES - 1)
            dy = (shr(c, LCO) + C - dz) & (C - 1)
        else:
            dz, dy, dc = c, shr(d, LCO), d & (CORES - 1)
        node = ((y + YS - dy) & (YS - 1)) * CORES + ((core + CORES - dc) & (CORES - 1))
        q = node * (C * NX) + ((z + C - dz) & (C - 1)) * NX + ((x + j) & (NX - 1))
        order = hot(col == r * Q + q)
        wait_for(XP.at[pl.ds(first_row, 4 * Q), pl.ds(0, QUADS * 2 * H)], ssem)
        NS = min(TILE, 2 * H)
        for p in range(QUADS):
            for i in range(2 * H // NS):
                cols = slice(p * 2 * H + i * NS, p * 2 * H + (i + 1) * NS)
                out = mm(order, XP[first_row : first_row + 4 * Q, cols]).astype(BF16)
                for g in range(K * NX):
                    at = g * BLK + p * 4 * G
                    saved[at : at + 4 * G, i * NS : (i + 1) * NS] = out[g * 4 * G : (g + 1) * 4 * G]

    def b_forward():
        h = T // 2
        wait_for(TB.at[pl.ds(3 * T, T)], tbr.at[0])
        remote(TB.at[pl.ds(3 * T, h)], TB.at[pl.ds(2 * T, h)], tbs, tbr.at[2], right)
        wait_for(TB.at[pl.ds(T, T)], tbr.at[1])
        remote(TB.at[pl.ds(T + h, h)], TB.at[pl.ds(2 * T + h, h)], tbs, tbr.at[2], left)

    def b_routes():
        wait_for(IDS.at[pl.ds(1, NX - 1)], idsr)
        return [own] + [route(IDS[j, :2]) for j in range(1, NX)]

    def b_part(ref, c, lead):
        lo = MB if c == 0 else 0
        return ref.at[lead, pl.ds(lo, ROWS - lo)] if lead is not None else ref.at[pl.ds(lo, ROWS - lo)]

    def b_select(c, routes):
        slot = c % NSB
        at = iota((ROWS, T), 0)
        parts = []
        for j in range(NX):
            part = jnp.zeros((ROWS, T), F32)
            for blk, rank in routes[j]:
                part += (at == (blk - c * G) * MB + j * SLOT + rank).astype(F32)
            parts.append(part)
            selT[j * T : (j + 1) * T, c * ROWS : (c + 1) * ROWS] = jnp.transpose(part).astype(BF16)
        sel = jnp.concatenate(parts, axis=1).astype(BF16)
        if c == 0:
            wait_for(TB.at[pl.ds(2 * T, T)], tbr.at[2])
        if c >= NSB and (G > 1 or c > NSB):
            wait_for(b_part(sendB, c - NSB, slot), sbs.at[slot])
        for i in range(DB // TILE):
            cols = slice(i * TILE, (i + 1) * TILE)
            sendB[slot, :, cols] = mm(sel, TB[:, cols]).astype(BF16)
        for d in range(G):
            if c or d:
                remote(
                    sendB.at[slot, pl.ds(d * MB, MB)], Y.at[pl.ds(c * ROWS + d * MB, MB), colsB],
                    sbs.at[slot], sbr.at[c], peer(c, d),
                )
            else:
                Y[:MB, DA:] = sendB[slot, :MB]

    def b_land(c):
        lo = MB if c == 0 else 0
        if ROWS > lo:
            wait_for(Y.at[pl.ds(c * ROWS + lo, ROWS - lo), colsB], sbr.at[c])
        rows = slice(c * ROWS, (c + 1) * ROWS)
        for i in range(DB // TILE):
            cols = slice(DA + i * TILE, DA + (i + 1) * TILE)
            Y[rows, cols] = mm(perm[...], Y[rows, cols]).astype(BF16)

    def yrows(c, j, lo=0, size=None):
        return pl.ds(c * ROWS + j * BLK + lo, BLK if size is None else size)

    def gather_start(c):
        lo = PAD if c == 0 else 0
        if MSG > lo:
            wait_for(recv.at[pl.ds(c * MSG + lo, MSG - lo)], s1r.at[c])
        own_rows = slice(c * ROWS, c * ROWS + BLK)
        for i in range(DA // TILE):
            cols = slice(i * TILE, (i + 1) * TILE)
            Y[own_rows, cols] = mm(compact, recv[c * MSG : (c + 1) * MSG, cols]).astype(BF16)
        GB[c, 0] = mm(gate_pick, recv[c * MSG : (c + 1) * MSG, :128]).astype(BF16)
        remote(Y.at[yrows(c, 0), colsA], Y.at[yrows(c, 3), colsA], ags, agr.at[c, 0], right)
        remote(Y.at[yrows(c, 0), colsA], Y.at[yrows(c, 1), colsA], ags, agr.at[c, 1], left)
        for k in range(1, NX):
            remote(GB.at[c, 0], GB.at[c, NX - k], gbs, gbr.at[c], along(k))

    def cut_of(c):
        return BLK * (2 - c % 2) // 3

    def gather_forward(c):
        wait_for(Y.at[yrows(c, 3), colsA], agr.at[c, 0])
        cut = cut_of(c)
        remote(Y.at[yrows(c, 3, 0, cut), colsA], Y.at[yrows(c, 2, 0, cut), colsA], ags, agr.at[c, 2], right)
        wait_for(Y.at[yrows(c, 1), colsA], agr.at[c, 1])
        rest = BLK - cut
        remote(Y.at[yrows(c, 1, cut, rest), colsA], Y.at[yrows(c, 2, cut, rest), colsA], ags, agr.at[c, 2], left)

    def compute(c):
        base = c % NSLOT * ROWS
        wait_for(Y.at[yrows(c, 2), colsA], agr.at[c, 2])
        wait_for(GB.at[c, pl.ds(1, NX - 1)], gbr.at[c])
        b_land(c)
        if c == 0:
            wd_copy.wait()
            wait_for(send.at[pl.ds(0, K * MSG - PAD), colsA], s1s)
        NT = min(TILE, H)
        for i in range(H // NT):
            dact[:, i * NT : (i + 1) * NT] = mm_nt(Y[c * ROWS : (c + 1) * ROWS, :], wd[i * NT : (i + 1) * NT, :])
        for j in range(NX):
            rows = slice(j * BLK, (j + 1) * BLK)
            at = c * ROWS + j * BLK
            a = saved[at : at + BLK, :H].astype(F32)
            b = saved[at : at + BLK, H:].astype(F32)
            da = dact[rows, :]
            spread = mm(of_source, GB[c, j])
            scale = jnp.sum(jnp.where(slot_mask, spread, 0.0), axis=1, keepdims=True)
            s = jax.nn.sigmoid(a)
            act = a * s
            hidden = act * b
            part = jnp.sum(hidden * da, axis=1, keepdims=True)
            parts = jnp.where(slot_mask, part, 0.0).astype(BF16)
            GPS[c, j] = mm(by_source, parts).astype(BF16)
            dh = scale * da
            dpre[rows, :H] = (dh * b * s * (1.0 + a * (1.0 - s))).astype(BF16)
            dpre[rows, H:] = (dh * act).astype(BF16)
            dact[rows, :] = scale * hidden
        for k in range(1, NX):
            remote(GPS.at[c, k], GPR.at[c, NX - k], gps, gpr.at[c], along(k))
        if c == 0:
            wgu_copy.wait()
        if c >= NSLOT:
            o = c - NSLOT
            wait_for(XP.at[pl.ds(base + BLK, ROWS - BLK), colsA], xps.at[o])
            lo = MB if o == 0 else 0
            if ROWS > lo:
                wait_for(XP.at[pl.ds(base + lo, ROWS - lo), colsB], xpbs.at[o])

        def tile_b(i, _):
            cols = pl.ds(pl.multiple_of(DA + i * TILE, TILE), TILE)
            XP[base : base + ROWS, cols] = mm(permT[...], mm_nt(dpre[...], wgu[cols, :]).astype(BF16)).astype(BF16)
            return 0

        lax.fori_loop(0, DB // TILE, tile_b, 0)
        for d in range(G):
            if c or d:
                remote(
                    XP.at[pl.ds(base + d * MB, MB), colsB], backB.at[pl.ds((c * G + d) * MB, MB)],
                    xpbs.at[c], bbr.at[c], source(c, d),
                )
            else:
                backB[:MB] = XP[base : base + MB, DA:]

        def tile_a(i, _):
            cols = pl.ds(pl.multiple_of(i * TILE, TILE), TILE)
            XP[base : base + ROWS, cols] = mm_nt(dpre[...], wgu[cols, :]).astype(BF16)
            return 0

        lax.fori_loop(0, DA // TILE, tile_a, 0)

        cut = cut_of(c)
        rest = BLK - cut

        def part_of(j, lo, size):
            return XP.at[pl.ds(base + j * BLK + lo, size), colsA]

        remote(part_of(2, 0, cut), RA.at[c, pl.ds(0, cut)], xps.at[c], rar.at[c, 0], right)
        remote(part_of(2, cut, rest), RA.at[c, pl.ds(cut, rest)], xps.at[c], rar.at[c, 1], left)
        remote(part_of(1, cut, rest), RB.at[c, 0, pl.ds(cut, rest)], xps.at[c], rbr.at[c, 0], right)
        remote(part_of(3, 0, cut), RB.at[c, 1, pl.ds(0, cut)], xps.at[c], rbr.at[c, 1], left)
        send[:H, c * ROWS : (c + 1) * ROWS] = jnp.transpose(dact[...]).astype(BF16)

    def reduce_middle(c):
        base = c % NSLOT * ROWS
        cut = cut_of(c)
        for side, j, lo, size, dev in ((0, 1, 0, cut, right), (1, 3, cut, BLK - cut, left)):
            wait_for(RA.at[c, pl.ds(lo, size)], rar.at[c, side])
            at = base + j * BLK + lo
            rows = slice(at, at + size)
            XP[rows, :DA] = (XP[rows, :DA].astype(F32) + RA[c, lo : lo + size].astype(F32)).astype(BF16)
            remote(XP.at[pl.ds(at, size), colsA], RB.at[c, side, pl.ds(lo, size)], xps.at[c], rbr.at[c, side], dev)

    def reduce_end(c):
        base = c % NSLOT * ROWS
        wait_for(GPR.at[c, pl.ds(1, NX - 1)], gpr.at[c])
        total = GPS[c, 0].astype(F32)
        for k in range(1, NX):
            total += GPR[c, k].astype(F32)
        high = total.astype(BF16)
        low = (total - high.astype(F32)).astype(BF16)
        up = iota((MSG, PAD), 0) - iota((MSG, PAD), 1) * PAD
        gate_back = mm(hot(up == SLOT), high) + mm(hot(up == SLOT + 1), low)
        wait_for(RB.at[c, 0], rbr.at[c, 0])
        wait_for(RB.at[c, 1], rbr.at[c, 1])
        msg = slice(c * MSG, (c + 1) * MSG)
        for i in range(DA // TILE):
            cols = slice(i * TILE, (i + 1) * TILE)
            whole = XP[base : base + BLK, cols].astype(F32) + RB[c, 0, :, cols].astype(F32) + RB[c, 1, :, cols].astype(F32)
            out = mm(expand, whole.astype(BF16))
            if i == 0:
                recv[msg, :128] = (out[:, :128] + gate_back).astype(BF16)
                recv[msg, 128:TILE] = out[:, 128:].astype(BF16)
            else:
                recv[msg, cols] = out.astype(BF16)
        for d in range(G):
            rows = pl.ds((c * G + d) * PAD, PAD)
            if c or d:
                remote(recv.at[rows], back.at[rows], rets, backr.at[c], source(c, d))
        if c == 0:
            back[:PAD] = recv[:PAD]

    def b_sum():
        for c in range(K):
            lo = MB if c == 0 else 0
            if ROWS > lo:
                wait_for(backB.at[pl.ds(c * ROWS + lo, ROWS - lo)], bbr.at[c])
        wait_for(TB.at[pl.ds(0, 3 * T)], tbs)
        for i in range(DB // TILE):
            cols = slice(i * TILE, (i + 1) * TILE)
            TB[:, cols] = mm(selT[...], backB[:, cols]).astype(BF16)
        h = T // 2
        remote(TB.at[pl.ds(2 * T, h)], RAB.at[0], pbs, rabr.at[0], right)
        remote(TB.at[pl.ds(2 * T + h, h)], RAB.at[1], pbs, rabr.at[1], left)
        remote(TB.at[pl.ds(T + h, h)], RBB.at[0, pl.ds(h, h)], pbs, rbbr.at[0], right)
        remote(TB.at[pl.ds(3 * T, h)], RBB.at[1, pl.ds(0, h)], pbs, rbbr.at[1], left)

    def b_middle():
        h = T // 2
        for side, j, lo, dev in ((0, 1, 0, right), (1, 3, h, left)):
            wait_for(RAB.at[side], rabr.at[side])
            rows = slice(j * T + lo, j * T + lo + h)
            TB[rows, :] = (TB[rows, :].astype(F32) + RAB[side].astype(F32)).astype(BF16)
            remote(TB.at[pl.ds(j * T + lo, h)], RBB.at[side, pl.ds(lo, h)], pbs, rbbr.at[side], dev)

    def b_end():
        wait_for(RBB.at[0], rbbr.at[0])
        wait_for(RBB.at[1], rbbr.at[1])
        ig_ref[:, DA:] = (TB[:T].astype(F32) + RBB[0].astype(F32) + RBB[1].astype(F32)).astype(BF16)

    tiles = D // TILE

    def weight_grad(first, last):
        def tile(i, _):
            cols = pl.ds(pl.multiple_of(i * TILE, TILE), TILE)
            dg_ref[:, cols] = mm(send[:H, : K * ROWS], Y[:, cols]).astype(BF16)
            return 0

        lax.fori_loop(first, last, tile, 0)

    b_forward()
    gather_start(0)
    routes = b_routes()
    for c in range(min(2, K)):
        b_select(c, routes)
    gather_start(1)
    gather_forward(0)
    for c in range(2, min(4, K)):
        b_select(c, routes)
    sort_saved()
    for s in range(2, K + 3):
        if s < K:
            gather_start(s)
        if 4 <= s + 2 < K:
            b_select(s + 2, routes)
        if s - 1 < K:
            gather_forward(s - 1)
        if 0 <= s - 3 < K:
            compute(s - 3)
        if 0 <= s - 4 < K:
            reduce_middle(s - 4)
        if 0 <= s - 5 < K:
            reduce_end(s - 5)
    part = tiles // 4
    weight_grad(0, part)
    reduce_middle(K - 1)
    weight_grad(part, 2 * part)
    reduce_end(K - 2)
    b_sum()
    reduce_end(K - 1)
    b_middle()
    weight_grad(2 * part, tiles)
    b_end()

    for c in range(K):
        lo = PAD if c == 0 else 0
        if MSG > lo:
            wait_for(back.at[pl.ds(c * MSG + lo, MSG - lo)], backr.at[c])
    for i in range(DA // TILE):
        cols = slice(i * TILE, (i + 1) * TILE)
        ig_ref[:, cols] = mm(mt[...], back[:, cols]).astype(BF16)
    back_gates = jnp.transpose(back[:, :128].astype(F32)).astype(BF16)
    for k, (blk, rank) in enumerate(own):
        at = slots - blk * PAD
        found = mm(back_gates, hot((at == SLOT) | (at == SLOT + 1)))
        gg_ref[k : k + 1, :] = jnp.sum(jnp.where(lane_slot == rank, found, 0.0), axis=0, keepdims=True)

    wait_for(recv.at[pl.ds(0, K * MSG - PAD)], rets)
    wait_for(Y.at[pl.ds(0, K * 3 * BLK), colsA], ags)
    wait_for(IDS.at[pl.ds(1, NX - 1)], idss)
    wait_for(TB.at[pl.ds(0, 3 * T)], pbs)
    for c in range(K):
        wait_for(GB.at[c, pl.ds(1, NX - 1)], gbs)
        wait_for(GPS.at[c, pl.ds(1, NX - 1)], gps)
    for c in range(max(0, K - NSB), K):
        lo = MB if c == 0 else 0
        if ROWS > lo:
            wait_for(sendB.at[c % NSB, pl.ds(lo, ROWS - lo)], sbs.at[c % NSB])
    for c in range(max(0, K - NSLOT), K):
        base = c % NSLOT * ROWS
        lo = MB if c == 0 else 0
        wait_for(XP.at[pl.ds(base + BLK, ROWS - BLK), colsA], xps.at[c])
        if ROWS > lo:
            wait_for(XP.at[pl.ds(base + lo, ROWS - lo), colsB], xpbs.at[c])


def body(out_grad, gates, expert_ids, saved_pre, w_gate_up, w_down):
    T, D = out_grad.shape
    B = lax.axis_size("node")
    C = lax.axis_size("local") // NX
    Q, SLOT = saved_pre.shape[1:3]
    H = w_down.shape[1]
    DA = split(D)
    DB = D - DA
    saved = jnp.transpose(saved_pre[0], (1, 0, 2))
    _, K, G, _ = plan(B, C)
    BLK, MSG = G * SLOT, G * PAD
    ROWS = NX * BLK
    NSLOT = min(6, K)
    NSB = min(4, K)
    vm = pl.BlockSpec(memory_space=pltpu.VMEM)
    anywhere = pl.BlockSpec(memory_space=pl.ANY)
    dma = pltpu.SemaphoreType.DMA
    ig, gg, dg = pl.pallas_call(
        functools.partial(kernel, B, C, SLOT, NSLOT),
        out_shape=(
            pltpu.VMEM((T, D), BF16),
            pltpu.VMEM((2, T), F32),
            pltpu.VMEM((H, D), BF16),
        ),
        in_specs=[vm, vm, anywhere, anywhere, anywhere, anywhere],
        out_specs=(vm, vm, vm),
        scratch_shapes=[
            pltpu.VMEM((T, D), BF16),
            pltpu.VMEM((D, 2 * H), BF16),
            pltpu.VMEM((max(K * MSG, H), max(DA, K * ROWS)), BF16),
            pltpu.VMEM((K * MSG, DA), BF16),
            pltpu.VMEM((K * MSG, DA), BF16),
            pltpu.VMEM((K * ROWS, D), BF16),
            pltpu.VMEM((K, NX, PAD, 128), BF16),
            pltpu.VMEM((NSLOT * ROWS, D), BF16),
            pltpu.VMEM((K, BLK, DA), BF16),
            pltpu.VMEM((K, 2, BLK, DA), BF16),
            pltpu.VMEM((K, NX, PAD, 128), BF16),
            pltpu.VMEM((K, NX, PAD, 128), BF16),
            pltpu.VMEM((K * ROWS, 2 * H), BF16),
            pltpu.VMEM((T, K * MSG), BF16),
            pltpu.VMEM((ROWS, 2 * H), BF16),
            pltpu.VMEM((ROWS, H), F32),
            pltpu.VMEM((NX, 8, T), jnp.int32),
            pltpu.VMEM((NX * T, DB), BF16),
            pltpu.VMEM((NSB, ROWS, DB), BF16),
            pltpu.VMEM((K * ROWS, DB), BF16),
            pltpu.VMEM((2, T // 2, DB), BF16),
            pltpu.VMEM((2, T, DB), BF16),
            pltpu.VMEM((NX * T, K * ROWS), BF16),
            pltpu.VMEM((ROWS, ROWS), BF16),
            pltpu.VMEM((ROWS, ROWS), BF16),
            dma((3,)),
            dma,
            dma,
            dma((K,)),
            dma,
            dma((K, 3)),
            dma,
            dma((K,)),
            dma((K,)),
            dma((K, 2)),
            dma((K, 2)),
            dma,
            dma((K,)),
            dma,
            dma((K,)),
            dma,
            dma,
            dma,
            dma((3,)),
            dma((NSB,)),
            dma((K,)),
            dma((K,)),
            dma((K,)),
            dma,
            dma((2,)),
            dma((2,)),
        ],
        compiler_params=pltpu.CompilerParams(
            collective_id=0, has_side_effects=True, vmem_limit_bytes=59 * 1024 * 1024
        ),
        cost_estimate=pl.CostEstimate(
            flops=2 * K * ROWS * D * 4 * H, bytes_accessed=25_000_000, transcendentals=K * ROWS * H
        ),
        name="moe_backward",
    )(expert_ids.T, gates.T, out_grad, saved, w_gate_up[0], w_down[0])
    return ig, gg.T, dg[None]


def solution(mesh):
    in_specs = (
        P(("node", "local"), None),
        P(("node", "local"), None),
        P(("node", "local"), None),
        P(("node", "local"), None, None, None),
        P(("node", "local"), None, None),
        P(("node", "local"), None, None),
    )
    out_specs = (
        P(("node", "local"), None),
        P(("node", "local"), None),
        P(("node", "local"), None, None),
    )
    return jax.shard_map(body, mesh=mesh, in_specs=in_specs, out_specs=out_specs, check_vma=False)
```

time: 194 us -> 185 us (0.954); the launches traced: 191 us -> 185 us
  local copies, waits for them, and re-layouts: 7.49 us -> 3.32 us
  Pallas kernels: 183 us -> 181 us
    unnamed x3, local copies, waits for them, and re-layouts: 7.49 us -> 3.32 us
where the time goes in v4:
time: 185 us
  Pallas kernels  181 us (98%)
  local copies, waits for them, and re-layouts  3.32 us (2%)
    pallas_call x1, Pallas kernels, body(): pl.pallas_call(functools.partial(kernel, B, C, SLOT, NSLOT), out_shape=(p...  181 us

profile of v4, /device:TPU:0, one launch (start us, length us, event | category | flops | bytes accessed | tf_op | source)
XLA Modules:
  0.0 185.3 jit_solution(2533975679775253671)
XLA Ops:
  0.6 181.4 %moe_backward.1 = (bf16[128,3584]{1,0:T(8,128)(2,1)S(1)}, f32[2,128]{1,0:T(2,128)S(1)}, bf16[512,3584]{1,0:T(8,128)(2,1)S(1)}) custom-call(s32[2,128]{1,0:T(2,128)} %bitcast.14, bf16[2,128]{1,0:T(2,128)(2,1)} %bitcast.15, bf16[128,3584]{1,0:T(8,128)(2,1)} %og_hbm.1, bf16[12,128,1024]{2,1,0:T(8,128)(2,1)} %bitcast.13, bf16[3584,1024]{1,0:T(8,128)(2,1)} %bitcast.11, ...), custom_call_target="tpu_custom_call" | custom-call | flops 22548578304 | bytes 25000000 | tf_op jit(solution)/shard_map/moe_backward/pallas_call | solution.py:548
  182.0 0.9 copy.12
  182.9 0.6 copy.13
  183.5 1.8 copy.14

commit v5 on v4

--- a/solution.py
+++ b/solution.py
@@ -16,7 +16,7 @@
 
 
 def split(D):
-    return max(TILE, 11 * D // 14 // TILE * TILE)
+    return max(512, 5 * D // 7 // 512 * 512)
 
 
 def iota(shape, dim):
@@ -64,6 +64,11 @@
     wd = dg_ref
     DA = split(D)
     DB = D - DA
+    SEG = DA // 4
+    segs = [slice(m * SEG, (m + 1) * SEG) for m in range(4)]
+    extra = slice(3 * SEG, 3 * SEG + 128)
+    W = 3 * SEG + 128
+    WIDE = 2 * TILE if DB % (2 * TILE) == 0 else TILE
     CORES, K, G, even = plan(B, C)
     BLK = G * SLOT
     MSG = G * PAD
@@ -71,7 +76,7 @@
     ROWS = NX * BLK
     NSB = sendB.shape[0]
     LG, LC = log2(G), log2(C)
-    colsA, colsB = pl.ds(0, DA), pl.ds(DA, DB)
+    colsA, colsB, colsW = pl.ds(0, DA), pl.ds(DA, DB), pl.ds(0, W)
     n = lax.axis_index("node")
     l = lax.axis_index("local")
     z, x = l // NX, l % NX
@@ -156,17 +161,25 @@
         return out
 
     own = route(ids_ref[...])
+    def third(v):
+        return shr(v * 11, 5)
+
     slots = iota((K * MSG, T), 0)
     lane_slot = iota((128, T), 0)
-    pick = jnp.zeros((K * MSG, T), F32)
+    picks = [jnp.zeros((K * MSG, T), F32) for _ in range(4)]
     gate_rows = jnp.zeros((K * MSG, 128), F32)
     gates = gates_ref[...].astype(F32)
     for k, (blk, rank) in enumerate(own):
-        pick += (slots == blk * PAD + rank).astype(F32)
+        at = slots - blk * PAD
+        picks[3] += (at == rank).astype(F32)
+        for m in range(3):
+            tail = jnp.where(rank - 3 * third(rank) == m, SLOT + third(rank), -K * MSG)
+            picks[m] += (at == tail).astype(F32)
         gate_at = jnp.where(lane_slot == rank, gates[k : k + 1], 0.0).astype(BF16)
-        gate_rows += mm_nt(hot(slots == blk * PAD + SLOT), gate_at)
-    mt[...] = jnp.transpose(pick).astype(BF16)
-    pick = pick.astype(BF16)
+        gate_rows += mm_nt(hot(at == 0), gate_at)
+    for m in range(4):
+        mt[m] = jnp.transpose(picks[m]).astype(BF16)
+    picks = [p.astype(BF16) for p in picks]
     og_copy.wait()
     TB[:T] = og_ref[:, DA:]
 
@@ -177,19 +190,24 @@
     remote(TB.at[pl.ds(0, T)], TB.at[pl.ds(3 * T, T)], tbs, tbr.at[0], right)
     remote(TB.at[pl.ds(0, T)], TB.at[pl.ds(T, T)], tbs, tbr.at[1], left)
 
-    HEAD = K // 4 if K >= 4 else K
-    for g in range(0, K, HEAD):
-        rows = slice(g * MSG, (g + HEAD) * MSG)
-        for i in range(DA // TILE):
-            cols = slice(i * TILE, (i + 1) * TILE)
-            send[rows, cols] = mm(pick[rows], og_ref[:, cols]).astype(BF16)
-        send[rows, :128] = (send[rows, :128].astype(F32) + gate_rows[rows]).astype(BF16)
-        for c in range(g, g + HEAD):
-            for d in range(G):
-                at = pl.ds((c * G + d) * PAD, PAD)
-                if c or d:
-                    remote(send.at[at, colsA], recv.at[at], s1s, s1r.at[c], peer(c, d))
-    recv[:PAD] = send[:PAD, :DA]
+    HEAD = max(1, K // 4)
+
+    def a_send(first, last):
+        for g in range(first, last, HEAD):
+            rows = slice(g * MSG, (g + HEAD) * MSG)
+            for m in range(3):
+                both = mm(picks[3][rows], og_ref[:, segs[m]]) + mm(picks[m][rows], og_ref[:, segs[3]])
+                send[rows, segs[m]] = both.astype(BF16)
+            send[rows, extra] = gate_rows[rows].astype(BF16)
+            for c in range(g, g + HEAD):
+                for d in range(G):
+                    at = pl.ds((c * G + d) * PAD, PAD)
+                    if c or d:
+                        remote(send.at[at, colsW], recv.at[at], s1s, s1r.at[c], peer(c, d))
+        if first == 0:
+            recv[:PAD] = send[:PAD, :W]
+
+    a_send(0, K // 2)
 
     def row_parts(i):
         j = jnp.zeros(i.shape, jnp.int32)
@@ -198,11 +216,15 @@
         rest = i - j * BLK
         return j, shr(rest, LG), rest & (G - 1)
 
-    _, r_i, d_i = row_parts(iota((BLK, MSG), 0))
-    compact = hot(iota((BLK, MSG), 1) == d_i * PAD + r_i)
-    _, r_l, d_l = row_parts(iota((MSG, BLK), 1))
-    expand = hot(iota((MSG, BLK), 0) == d_l * PAD + r_l)
-    gate_pick = hot(iota((PAD, MSG), 1) == iota((PAD, MSG), 0) * PAD + SLOT)
+    def places(shape, dim):
+        _, r, d = row_parts(iota(shape, dim))
+        at = iota(shape, 1 - dim) - d * PAD
+        tails = [hot((at == SLOT + third(r)) & (r - 3 * third(r) == m)) for m in range(3)]
+        return tails + [hot(at == r)]
+
+    compact = places((BLK, MSG), 0)
+    expand = places((MSG, BLK), 1)
+    gate_pick = hot(iota((PAD, MSG), 1) == iota((PAD, MSG), 0) * PAD)
     of_source = hot((iota((BLK, PAD), 0) & (G - 1)) == iota((BLK, PAD), 1))
     by_source = hot((iota((PAD, BLK), 1) & (G - 1)) == iota((PAD, BLK), 0))
     slot_mask = iota((BLK, 128), 1) == shr(iota((BLK, 128), 0), LG)
@@ -291,10 +313,13 @@
         if MSG > lo:
             wait_for(recv.at[pl.ds(c * MSG + lo, MSG - lo)], s1r.at[c])
         own_rows = slice(c * ROWS, c * ROWS + BLK)
-        for i in range(DA // TILE):
-            cols = slice(i * TILE, (i + 1) * TILE)
-            Y[own_rows, cols] = mm(compact, recv[c * MSG : (c + 1) * MSG, cols]).astype(BF16)
-        GB[c, 0] = mm(gate_pick, recv[c * MSG : (c + 1) * MSG, :128]).astype(BF16)
+        msg = slice(c * MSG, (c + 1) * MSG)
+        last = jnp.zeros((BLK, SEG), F32)
+        for m in range(3):
+            Y[own_rows, segs[m]] = mm(compact[3], recv[msg, segs[m]]).astype(BF16)
+            last += mm(compact[m], recv[msg, segs[m]])
+        Y[own_rows, segs[3]] = last.astype(BF16)
+        GB[c, 0] = mm(gate_pick, recv[msg, extra]).astype(BF16)
         remote(Y.at[yrows(c, 0), colsA], Y.at[yrows(c, 3), colsA], ags, agr.at[c, 0], right)
         remote(Y.at[yrows(c, 0), colsA], Y.at[yrows(c, 1), colsA], ags, agr.at[c, 1], left)
         for k in range(1, NX):
@@ -318,7 +343,6 @@
         b_land(c)
         if c == 0:
             wd_copy.wait()
-            wait_for(send.at[pl.ds(0, K * MSG - PAD), colsA], s1s)
         NT = min(TILE, H)
         for i in range(H // NT):
             dact[:, i * NT : (i + 1) * NT] = mm_nt(Y[c * ROWS : (c + 1) * ROWS, :], wd[i * NT : (i + 1) * NT, :])
@@ -352,11 +376,11 @@
                 wait_for(XP.at[pl.ds(base + lo, ROWS - lo), colsB], xpbs.at[o])
 
         def tile_b(i, _):
-            cols = pl.ds(pl.multiple_of(DA + i * TILE, TILE), TILE)
+            cols = pl.ds(pl.multiple_of(DA + i * WIDE, TILE), WIDE)
             XP[base : base + ROWS, cols] = mm(permT[...], mm_nt(dpre[...], wgu[cols, :]).astype(BF16)).astype(BF16)
             return 0
 
-        lax.fori_loop(0, DB // TILE, tile_b, 0)
+        lax.fori_loop(0, DB // WIDE, tile_b, 0)
         for d in range(G):
             if c or d:
                 remote(
@@ -367,11 +391,11 @@
                 backB[:MB] = XP[base : base + MB, DA:]
 
         def tile_a(i, _):
-            cols = pl.ds(pl.multiple_of(i * TILE, TILE), TILE)
+            cols = pl.ds(pl.multiple_of(i * WIDE, TILE), WIDE)
             XP[base : base + ROWS, cols] = mm_nt(dpre[...], wgu[cols, :]).astype(BF16)
             return 0
 
-        lax.fori_loop(0, DA // TILE, tile_a, 0)
+        lax.fori_loop(0, DA // WIDE, tile_a, 0)
 
         cut = cut_of(c)
         rest = BLK - cut
@@ -383,6 +407,8 @@
         remote(part_of(2, cut, rest), RA.at[c, pl.ds(cut, rest)], xps.at[c], rar.at[c, 1], left)
         remote(part_of(1, cut, rest), RB.at[c, 0, pl.ds(cut, rest)], xps.at[c], rbr.at[c, 0], right)
         remote(part_of(3, 0, cut), RB.at[c, 1, pl.ds(0, cut)], xps.at[c], rbr.at[c, 1], left)
+        if c == 0:
+            wait_for(send.at[pl.ds(0, K * MSG - PAD), colsW], s1s)
         send[:H, c * ROWS : (c + 1) * ROWS] = jnp.transpose(dact[...]).astype(BF16)
 
     def reduce_middle(c):
@@ -404,19 +430,18 @@
         high = total.astype(BF16)
         low = (total - high.astype(F32)).astype(BF16)
         up = iota((MSG, PAD), 0) - iota((MSG, PAD), 1) * PAD
-        gate_back = mm(hot(up == SLOT), high) + mm(hot(up == SLOT + 1), low)
+        gate_back = mm(hot(up == 0), high) + mm(hot(up == 1), low)
         wait_for(RB.at[c, 0], rbr.at[c, 0])
         wait_for(RB.at[c, 1], rbr.at[c, 1])
         msg = slice(c * MSG, (c + 1) * MSG)
-        for i in range(DA // TILE):
-            cols = slice(i * TILE, (i + 1) * TILE)
-            whole = XP[base : base + BLK, cols].astype(F32) + RB[c, 0, :, cols].astype(F32) + RB[c, 1, :, cols].astype(F32)
-            out = mm(expand, whole.astype(BF16))
-            if i == 0:
-                recv[msg, :128] = (out[:, :128] + gate_back).astype(BF16)
-                recv[msg, 128:TILE] = out[:, 128:].astype(BF16)
-            else:
-                recv[msg, cols] = out.astype(BF16)
+        def whole(cols):
+            part = XP[base : base + BLK, cols].astype(F32) + RB[c, 0, :, cols].astype(F32)
+            return (part + RB[c, 1, :, cols].astype(F32)).astype(BF16)
+
+        last = whole(segs[3])
+        for m in range(3):
+            recv[msg, segs[m]] = (mm(expand[3], whole(segs[m])) + mm(expand[m], last)).astype(BF16)
+        recv[msg, extra] = gate_back.astype(BF16)
         for d in range(G):
             rows = pl.ds((c * G + d) * PAD, PAD)
             if c or d:
@@ -452,11 +477,11 @@
         wait_for(RBB.at[1], rbbr.at[1])
         ig_ref[:, DA:] = (TB[:T].astype(F32) + RBB[0].astype(F32) + RBB[1].astype(F32)).astype(BF16)
 
-    tiles = D // TILE
+    tiles = D // WIDE
 
     def weight_grad(first, last):
         def tile(i, _):
-            cols = pl.ds(pl.multiple_of(i * TILE, TILE), TILE)
+            cols = pl.ds(pl.multiple_of(i * WIDE, TILE), WIDE)
             dg_ref[:, cols] = mm(send[:H, : K * ROWS], Y[:, cols]).astype(BF16)
             return 0
 
@@ -465,8 +490,9 @@
     b_forward()
     gather_start(0)
     routes = b_routes()
-    for c in range(min(2, K)):
-        b_select(c, routes)
+    b_select(0, routes)
+    b_select(1, routes)
+    a_send(K // 2, K)
     gather_start(1)
     gather_forward(0)
     for c in range(2, min(4, K)):
@@ -485,28 +511,30 @@
             reduce_middle(s - 4)
         if 0 <= s - 5 < K:
             reduce_end(s - 5)
-    part = tiles // 4
+    part = tiles // 3
     weight_grad(0, part)
     reduce_middle(K - 1)
+    b_sum()
+    reduce_end(K - 2)
     weight_grad(part, 2 * part)
-    reduce_end(K - 2)
-    b_sum()
     reduce_end(K - 1)
+    weight_grad(2 * part, tiles)
     b_middle()
-    weight_grad(2 * part, tiles)
     b_end()
 
     for c in range(K):
         lo = PAD if c == 0 else 0
         if MSG > lo:
             wait_for(back.at[pl.ds(c * MSG + lo, MSG - lo)], backr.at[c])
-    for i in range(DA // TILE):
-        cols = slice(i * TILE, (i + 1) * TILE)
-        ig_ref[:, cols] = mm(mt[...], back[:, cols]).astype(BF16)
-    back_gates = jnp.transpose(back[:, :128].astype(F32)).astype(BF16)
+    last = jnp.zeros((T, SEG), F32)
+    for m in range(3):
+        ig_ref[:, segs[m]] = mm(mt[3], back[:, segs[m]]).astype(BF16)
+        last += mm(mt[m], back[:, segs[m]])
+    ig_ref[:, segs[3]] = last.astype(BF16)
+    back_gates = jnp.transpose(back[:, extra].astype(F32)).astype(BF16)
     for k, (blk, rank) in enumerate(own):
         at = slots - blk * PAD
-        found = mm(back_gates, hot((at == SLOT) | (at == SLOT + 1)))
+        found = mm(back_gates, hot((at == 0) | (at == 1)))
         gg_ref[k : k + 1, :] = jnp.sum(jnp.where(lane_slot == rank, found, 0.0), axis=0, keepdims=True)
 
     wait_for(recv.at[pl.ds(0, K * MSG - PAD)], rets)
@@ -535,13 +563,13 @@
     Q, SLOT = saved_pre.shape[1:3]
     H = w_down.shape[1]
     DA = split(D)
-    DB = D - DA
+    DB, W = D - DA, 3 * DA // 4 + 128
     saved = jnp.transpose(saved_pre[0], (1, 0, 2))
     _, K, G, _ = plan(B, C)
     BLK, MSG = G * SLOT, G * PAD
     ROWS = NX * BLK
     NSLOT = min(6, K)
-    NSB = min(4, K)
+    NSB = K
     vm = pl.BlockSpec(memory_space=pltpu.VMEM)
     anywhere = pl.BlockSpec(memory_space=pl.ANY)
     dma = pltpu.SemaphoreType.DMA
@@ -557,9 +585,9 @@
         scratch_shapes=[
             pltpu.VMEM((T, D), BF16),
             pltpu.VMEM((D, 2 * H), BF16),
-            pltpu.VMEM((max(K * MSG, H), max(DA, K * ROWS)), BF16),
-            pltpu.VMEM((K * MSG, DA), BF16),
-            pltpu.VMEM((K * MSG, DA), BF16),
+            pltpu.VMEM((max(K * MSG, H), max(W, K * ROWS)), BF16),
+            pltpu.VMEM((K * MSG, W), BF16),
+            pltpu.VMEM((K * MSG, W), BF16),
             pltpu.VMEM((K * ROWS, D), BF16),
             pltpu.VMEM((K, NX, PAD, 128), BF16),
             pltpu.VMEM((NSLOT * ROWS, D), BF16),
@@ -568,7 +596,7 @@
             pltpu.VMEM((K, NX, PAD, 128), BF16),
             pltpu.VMEM((K, NX, PAD, 128), BF16),
             pltpu.VMEM((K * ROWS, 2 * H), BF16),
-            pltpu.VMEM((T, K * MSG), BF16),
+            pltpu.VMEM((4, T, K * MSG), BF16),
             pltpu.VMEM((ROWS, 2 * H), BF16),
             pltpu.VMEM((ROWS, H), F32),
             pltpu.VMEM((NX, 8, T), jnp.int32),

time: 185 us -> 168 us (0.908)
  Pallas kernels: 181 us -> 164 us
    pallas_call x1, Pallas kernels: 181 us -> 164 us  [body(): pl.pallas_call(functools.partial(kernel, B, C, SLOT, NSLOT), out_shape=(p...]
where the time goes in v5:
time: 168 us
  Pallas kernels  164 us (98%)
  local copies, waits for them, and re-layouts  3.32 us (2%)
    pallas_call x1, Pallas kernels, body(): pl.pallas_call(functools.partial(kernel, B, C, SLOT, NSLOT), out_shape=(p...  164 us

profile of v5, /device:TPU:0, one launch (start us, length us, event | category | flops | bytes accessed | tf_op | source)
XLA Modules:
  0.0 167.8 jit_solution(16971154283856409645)
XLA Ops:
  0.6 163.8 %moe_backward.1 = (bf16[128,3584]{1,0:T(8,128)(2,1)S(1)}, f32[2,128]{1,0:T(2,128)S(1)}, bf16[512,3584]{1,0:T(8,128)(2,1)S(1)}) custom-call(s32[2,128]{1,0:T(2,128)} %bitcast.14, bf16[2,128]{1,0:T(2,128)(2,1)} %bitcast.15, bf16[128,3584]{1,0:T(8,128)(2,1)} %og_hbm.1, bf16[12,128,1024]{2,1,0:T(8,128)(2,1)} %bitcast.13, bf16[3584,1024]{1,0:T(8,128)(2,1)} %bitcast.11, ...), custom_call_target="tpu_custom_call" | custom-call | flops 22548578304 | bytes 25000000 | tf_op jit(solution)/shard_map/moe_backward/pallas_call | solution.py:576
  164.5 0.9 copy.12
  165.4 0.6 copy.13
  166.0 1.8 %copy.14 = bf16[1,512,3584]{2,1,0:T(8,128)(2,1)} copy(bf16[1,512,3584]{2,1,0:T(8,128)(2,1)S(1)} %bitcast.9) | data formatting | bytes 7340032

commit v6 on v5

--- a/solution.py
+++ b/solution.py
@@ -16,7 +16,11 @@
 
 
 def split(D):
-    return max(512, 5 * D // 7 // 512 * 512)
+    return max(3 * TILE, 9 * D // 14 // TILE * TILE)
+
+
+def spare_columns(DA):
+    return (DA - 128) // 4 // 128 * 128
 
 
 def iota(shape, dim):
@@ -54,7 +58,7 @@
     B, C, SLOT, NSLOT,
     ids_ref, gates_ref, og_hbm, saved_hbm, wgu_hbm, wd_hbm,
     ig_ref, gg_ref, dg_ref,
-    og_ref, wgu, send, recv, back, Y, GB, XP, RA, RB, GPS, GPR, saved, mt, dpre, dact,
+    og_ref, wgu, send, recv, back, Y, GB, XP, RA, RB, GPS, GPR, saved, wT, mt, dpre, dact,
     IDS, TB, sendB, backB, RAB, RBB, selT, perm, permT,
     wsem, ssem, s1s, s1r, ags, agr, gbs, gbr, xps, rar, rbr, gps, gpr, rets, backr,
     idss, idsr, tbs, tbr, sbs, sbr, xpbs, bbr, pbs, rabr, rbbr,
@@ -64,11 +68,14 @@
     wd = dg_ref
     DA = split(D)
     DB = D - DA
-    SEG = DA // 4
-    segs = [slice(m * SEG, (m + 1) * SEG) for m in range(4)]
-    extra = slice(3 * SEG, 3 * SEG + 128)
-    W = 3 * SEG + 128
-    WIDE = 2 * TILE if DB % (2 * TILE) == 0 else TILE
+    S = spare_columns(DA)
+    W = DA - S
+    segs = [slice(m * S, (m + 1) * S) for m in range(3)] + [slice(3 * S, W)]
+    tail = slice(W, DA)
+    extra = slice(3 * S, 3 * S + 128)
+    WA = 3 * TILE if DA % (3 * TILE) == 0 else TILE
+    WB = DB // 2 if DB % 256 == 0 else DB
+    WG = 2 * TILE
     CORES, K, G, even = plan(B, C)
     BLK = G * SLOT
     MSG = G * PAD
@@ -76,7 +83,7 @@
     ROWS = NX * BLK
     NSB = sendB.shape[0]
     LG, LC = log2(G), log2(C)
-    colsA, colsB, colsW = pl.ds(0, DA), pl.ds(DA, DB), pl.ds(0, W)
+    colsA, colsB = pl.ds(0, DA), pl.ds(DA, DB)
     n = lax.axis_index("node")
     l = lax.axis_index("local")
     z, x = l // NX, l % NX
@@ -139,6 +146,12 @@
     wgu_copy.start()
 
     IDS[0, :2] = ids_ref[...]
+    pl.semaphore_wait(barrier, count)
+    remote(og_hbm.at[:, colsB], TB.at[pl.ds(3 * T, T)], tbs, tbr.at[0], right)
+    remote(og_hbm.at[:, colsB], TB.at[pl.ds(T, T)], tbs, tbr.at[1], left)
+    for k in range(1, NX):
+        remote(IDS.at[0], IDS.at[NX - k], idss, idsr, along(k))
+
     NE = max(8, B * C)
     before = hot(iota((T, T), 0) < iota((T, T), 1))
     expert_row = iota((NE, T), 0)
@@ -173,22 +186,13 @@
         at = slots - blk * PAD
         picks[3] += (at == rank).astype(F32)
         for m in range(3):
-            tail = jnp.where(rank - 3 * third(rank) == m, SLOT + third(rank), -K * MSG)
-            picks[m] += (at == tail).astype(F32)
+            spare = jnp.where(rank - 3 * third(rank) == m, SLOT + third(rank), -K * MSG)
+            picks[m] += (at == spare).astype(F32)
         gate_at = jnp.where(lane_slot == rank, gates[k : k + 1], 0.0).astype(BF16)
-        gate_rows += mm_nt(hot(at == 0), gate_at)
-    for m in range(4):
-        mt[m] = jnp.transpose(picks[m]).astype(BF16)
+        gate_rows += mm_nt(hot(at == SLOT), gate_at)
+    picks_t = [jnp.transpose(p).astype(BF16) for p in picks]
     picks = [p.astype(BF16) for p in picks]
     og_copy.wait()
-    TB[:T] = og_ref[:, DA:]
-
-    pl.semaphore_wait(barrier, count)
-
-    for k in range(1, NX):
-        remote(IDS.at[0], IDS.at[NX - k], idss, idsr, along(k))
-    remote(TB.at[pl.ds(0, T)], TB.at[pl.ds(3 * T, T)], tbs, tbr.at[0], right)
-    remote(TB.at[pl.ds(0, T)], TB.at[pl.ds(T, T)], tbs, tbr.at[1], left)
 
     HEAD = max(1, K // 4)
 
@@ -196,18 +200,23 @@
         for g in range(first, last, HEAD):
             rows = slice(g * MSG, (g + HEAD) * MSG)
             for m in range(3):
-                both = mm(picks[3][rows], og_ref[:, segs[m]]) + mm(picks[m][rows], og_ref[:, segs[3]])
+                both = mm(picks[3][rows], og_ref[:, segs[m]]) + mm(picks[m][rows], og_ref[:, tail])
                 send[rows, segs[m]] = both.astype(BF16)
-            send[rows, extra] = gate_rows[rows].astype(BF16)
+            rest = mm(picks[3][rows], og_ref[:, segs[3]])
+            rest = jnp.concatenate([rest[:, :128] + gate_rows[rows], rest[:, 128:]], axis=1)
+            send[rows, segs[3]] = rest.astype(BF16)
             for c in range(g, g + HEAD):
                 for d in range(G):
                     at = pl.ds((c * G + d) * PAD, PAD)
                     if c or d:
-                        remote(send.at[at, colsW], recv.at[at], s1s, s1r.at[c], peer(c, d))
+                        remote(send.at[at], recv.at[at], s1s, s1r.at[c], peer(c, d))
         if first == 0:
-            recv[:PAD] = send[:PAD, :W]
+            recv[:PAD] = send[:PAD]
 
     a_send(0, K // 2)
+    TB[:T] = og_ref[:, DA:]
+    for m in range(4):
+        mt[m] = picks_t[m]
 
     def row_parts(i):
         j = jnp.zeros(i.shape, jnp.int32)
@@ -224,7 +233,7 @@
 
     compact = places((BLK, MSG), 0)
     expand = places((MSG, BLK), 1)
-    gate_pick = hot(iota((PAD, MSG), 1) == iota((PAD, MSG), 0) * PAD)
+    gate_pick = hot(iota((PAD, MSG), 1) == iota((PAD, MSG), 0) * PAD + SLOT)
     of_source = hot((iota((BLK, PAD), 0) & (G - 1)) == iota((BLK, PAD), 1))
     by_source = hot((iota((PAD, BLK), 1) & (G - 1)) == iota((PAD, BLK), 0))
     slot_mask = iota((BLK, 128), 1) == shr(iota((BLK, 128), 0), LG)
@@ -314,11 +323,12 @@
             wait_for(recv.at[pl.ds(c * MSG + lo, MSG - lo)], s1r.at[c])
         own_rows = slice(c * ROWS, c * ROWS + BLK)
         msg = slice(c * MSG, (c + 1) * MSG)
-        last = jnp.zeros((BLK, SEG), F32)
-        for m in range(3):
+        last = jnp.zeros((BLK, S), F32)
+        for m in range(4):
             Y[own_rows, segs[m]] = mm(compact[3], recv[msg, segs[m]]).astype(BF16)
-            last += mm(compact[m], recv[msg, segs[m]])
-        Y[own_rows, segs[3]] = last.astype(BF16)
+            if m < 3:
+                last += mm(compact[m], recv[msg, segs[m]])
+        Y[own_rows, tail] = last.astype(BF16)
         GB[c, 0] = mm(gate_pick, recv[msg, extra]).astype(BF16)
         remote(Y.at[yrows(c, 0), colsA], Y.at[yrows(c, 3), colsA], ags, agr.at[c, 0], right)
         remote(Y.at[yrows(c, 0), colsA], Y.at[yrows(c, 1), colsA], ags, agr.at[c, 1], left)
@@ -376,11 +386,11 @@
                 wait_for(XP.at[pl.ds(base + lo, ROWS - lo), colsB], xpbs.at[o])
 
         def tile_b(i, _):
-            cols = pl.ds(pl.multiple_of(DA + i * WIDE, TILE), WIDE)
+            cols = pl.ds(pl.multiple_of(DA + i * WB, 128), WB)
             XP[base : base + ROWS, cols] = mm(permT[...], mm_nt(dpre[...], wgu[cols, :]).astype(BF16)).astype(BF16)
             return 0
 
-        lax.fori_loop(0, DB // WIDE, tile_b, 0)
+        lax.fori_loop(0, DB // WB, tile_b, 0)
         for d in range(G):
             if c or d:
                 remote(
@@ -391,11 +401,11 @@
                 backB[:MB] = XP[base : base + MB, DA:]
 
         def tile_a(i, _):
-            cols = pl.ds(pl.multiple_of(i * WIDE, TILE), WIDE)
+            cols = pl.ds(pl.multiple_of(i * WA, TILE), WA)
             XP[base : base + ROWS, cols] = mm_nt(dpre[...], wgu[cols, :]).astype(BF16)
             return 0
 
-        lax.fori_loop(0, DA // WIDE, tile_a, 0)
+        lax.fori_loop(0, DA // WA, tile_a, 0)
 
         cut = cut_of(c)
         rest = BLK - cut
@@ -407,9 +417,7 @@
         remote(part_of(2, cut, rest), RA.at[c, pl.ds(cut, rest)], xps.at[c], rar.at[c, 1], left)
         remote(part_of(1, cut, rest), RB.at[c, 0, pl.ds(cut, rest)], xps.at[c], rbr.at[c, 0], right)
         remote(part_of(3, 0, cut), RB.at[c, 1, pl.ds(0, cut)], xps.at[c], rbr.at[c, 1], left)
-        if c == 0:
-            wait_for(send.at[pl.ds(0, K * MSG - PAD), colsW], s1s)
-        send[:H, c * ROWS : (c + 1) * ROWS] = jnp.transpose(dact[...]).astype(BF16)
+        wT[:, c * ROWS : (c + 1) * ROWS] = jnp.transpose(dact[...]).astype(BF16)
 
     def reduce_middle(c):
         base = c % NSLOT * ROWS
@@ -430,7 +438,7 @@
         high = total.astype(BF16)
         low = (total - high.astype(F32)).astype(BF16)
         up = iota((MSG, PAD), 0) - iota((MSG, PAD), 1) * PAD
-        gate_back = mm(hot(up == 0), high) + mm(hot(up == 1), low)
+        gate_back = mm(hot(up == SLOT), high) + mm(hot(up == SLOT + 1), low)
         wait_for(RB.at[c, 0], rbr.at[c, 0])
         wait_for(RB.at[c, 1], rbr.at[c, 1])
         msg = slice(c * MSG, (c + 1) * MSG)
@@ -438,10 +446,12 @@
             part = XP[base : base + BLK, cols].astype(F32) + RB[c, 0, :, cols].astype(F32)
             return (part + RB[c, 1, :, cols].astype(F32)).astype(BF16)
 
-        last = whole(segs[3])
+        last = whole(tail)
         for m in range(3):
             recv[msg, segs[m]] = (mm(expand[3], whole(segs[m])) + mm(expand[m], last)).astype(BF16)
-        recv[msg, extra] = gate_back.astype(BF16)
+        rest = mm(expand[3], whole(segs[3]))
+        rest = jnp.concatenate([rest[:, :128] + gate_back, rest[:, 128:]], axis=1)
+        recv[msg, segs[3]] = rest.astype(BF16)
         for d in range(G):
             rows = pl.ds((c * G + d) * PAD, PAD)
             if c or d:
@@ -477,12 +487,12 @@
         wait_for(RBB.at[1], rbbr.at[1])
         ig_ref[:, DA:] = (TB[:T].astype(F32) + RBB[0].astype(F32) + RBB[1].astype(F32)).astype(BF16)
 
-    tiles = D // WIDE
+    tiles = D // WG
 
     def weight_grad(first, last):
         def tile(i, _):
-            cols = pl.ds(pl.multiple_of(i * WIDE, TILE), WIDE)
-            dg_ref[:, cols] = mm(send[:H, : K * ROWS], Y[:, cols]).astype(BF16)
+            cols = pl.ds(pl.multiple_of(i * WG, TILE), WG)
+            dg_ref[:, cols] = mm(wT[...], Y[:, cols]).astype(BF16)
             return 0
 
         lax.fori_loop(first, last, tile, 0)
@@ -498,27 +508,35 @@
     for c in range(2, min(4, K)):
         b_select(c, routes)
     sort_saved()
-    for s in range(2, K + 3):
-        if s < K:
-            gather_start(s)
-        if 4 <= s + 2 < K:
-            b_select(s + 2, routes)
-        if s - 1 < K:
-            gather_forward(s - 1)
-        if 0 <= s - 3 < K:
-            compute(s - 3)
-        if 0 <= s - 4 < K:
-            reduce_middle(s - 4)
-        if 0 <= s - 5 < K:
-            reduce_end(s - 5)
+    for c in range(2, min(4, K)):
+        gather_start(c)
+        if c == 2:
+            gather_forward(1)
+    if K == 2:
+        gather_forward(1)
+    for c in range(4, K):
+        b_select(c, routes)
+    ended = 0
+    for c in range(K):
+        compute(c)
+        if c + 2 < K:
+            gather_forward(c + 2)
+        if c + 4 < K:
+            gather_start(c + 4)
+        if c >= 1:
+            reduce_middle(c - 1)
+        done = c - 2 if c > K // 2 else c - 3
+        for o in range(ended, done + 1):
+            reduce_end(o)
+        ended = max(ended, done + 1)
     part = tiles // 3
     weight_grad(0, part)
     reduce_middle(K - 1)
+    for o in range(ended, K - 1):
+        reduce_end(o)
     b_sum()
-    reduce_end(K - 2)
-    weight_grad(part, 2 * part)
+    weight_grad(part, tiles)
     reduce_end(K - 1)
-    weight_grad(2 * part, tiles)
     b_middle()
     b_end()
 
@@ -526,17 +544,19 @@
         lo = PAD if c == 0 else 0
         if MSG > lo:
             wait_for(back.at[pl.ds(c * MSG + lo, MSG - lo)], backr.at[c])
-    last = jnp.zeros((T, SEG), F32)
-    for m in range(3):
+    last = jnp.zeros((T, S), F32)
+    for m in range(4):
         ig_ref[:, segs[m]] = mm(mt[3], back[:, segs[m]]).astype(BF16)
-        last += mm(mt[m], back[:, segs[m]])
-    ig_ref[:, segs[3]] = last.astype(BF16)
+        if m < 3:
+            last += mm(mt[m], back[:, segs[m]])
+    ig_ref[:, tail] = last.astype(BF16)
     back_gates = jnp.transpose(back[:, extra].astype(F32)).astype(BF16)
     for k, (blk, rank) in enumerate(own):
         at = slots - blk * PAD
-        found = mm(back_gates, hot((at == 0) | (at == 1)))
+        found = mm(back_gates, hot((at == SLOT) | (at == SLOT + 1)))
         gg_ref[k : k + 1, :] = jnp.sum(jnp.where(lane_slot == rank, found, 0.0), axis=0, keepdims=True)
 
+    wait_for(send.at[pl.ds(0, K * MSG - PAD)], s1s)
     wait_for(recv.at[pl.ds(0, K * MSG - PAD)], rets)
     wait_for(Y.at[pl.ds(0, K * 3 * BLK), colsA], ags)
     wait_for(IDS.at[pl.ds(1, NX - 1)], idss)
@@ -563,7 +583,7 @@
     Q, SLOT = saved_pre.shape[1:3]
     H = w_down.shape[1]
     DA = split(D)
-    DB, W = D - DA, 3 * DA // 4 + 128
+    DB, W = D - DA, DA - spare_columns(DA)
     saved = jnp.transpose(saved_pre[0], (1, 0, 2))
     _, K, G, _ = plan(B, C)
     BLK, MSG = G * SLOT, G * PAD
@@ -585,7 +605,7 @@
         scratch_shapes=[
             pltpu.VMEM((T, D), BF16),
             pltpu.VMEM((D, 2 * H), BF16),
-            pltpu.VMEM((max(K * MSG, H), max(W, K * ROWS)), BF16),
+            pltpu.VMEM((K * MSG, W), BF16),
             pltpu.VMEM((K * MSG, W), BF16),
             pltpu.VMEM((K * MSG, W), BF16),
             pltpu.VMEM((K * ROWS, D), BF16),
@@ -596,6 +616,7 @@
             pltpu.VMEM((K, NX, PAD, 128), BF16),
             pltpu.VMEM((K, NX, PAD, 128), BF16),
             pltpu.VMEM((K * ROWS, 2 * H), BF16),
+            pltpu.VMEM((H, K * ROWS), BF16),
             pltpu.VMEM((4, T, K * MSG), BF16),
             pltpu.VMEM((ROWS, 2 * H), BF16),
             pltpu.VMEM((ROWS, H), F32),

time: 168 us -> 166 us (0.988)
  Pallas kernels: 164 us -> 162 us
    pallas_call x1, Pallas kernels: 164 us -> 162 us  [body(): pl.pallas_call(functools.partial(kernel, B, C, SLOT, NSLOT), out_shape=(p...]
where the time goes in v6:
time: 166 us
  Pallas kernels  162 us (98%)
  local copies, waits for them, and re-layouts  3.32 us (2%)
    pallas_call x1, Pallas kernels, body(): pl.pallas_call(functools.partial(kernel, B, C, SLOT, NSLOT), out_shape=(p...  162 us
    unnamed x3, local copies, waits for them, and re-layouts  3.32 us

profile of v6, /device:TPU:0, one launch (start us, length us, event | category | flops | bytes accessed | tf_op | source)
XLA Modules:
  0.0 165.6 jit_solution(5997013110179756059)
XLA Ops:
  0.6 161.6 %moe_backward.1 = (bf16[128,3584]{1,0:T(8,128)(2,1)S(1)}, f32[2,128]{1,0:T(2,128)S(1)}, bf16[512,3584]{1,0:T(8,128)(2,1)S(1)}) custom-call(s32[2,128]{1,0:T(2,128)} %bitcast.14, bf16[2,128]{1,0:T(2,128)(2,1)} %bitcast.15, bf16[128,3584]{1,0:T(8,128)(2,1)} %og_hbm.1, bf16[12,128,1024]{2,1,0:T(8,128)(2,1)} %bitcast.13, bf16[3584,1024]{1,0:T(8,128)(2,1)} %bitcast.11, ...), custom_call_target="tpu_custom_call" | custom-call | flops 22548578304 | bytes 25000000 | tf_op jit(solution)/shard_map/moe_backward/pallas_call | solution.py:596
  162.3 0.9 copy.12
  163.2 0.6 copy.13
  163.8 1.8 %copy.14 = bf16[1,512,3584]{2,1,0:T(8,128)(2,1)} copy(bf16[1,512,3584]{2,1,0:T(8,128)(2,1)S(1)} %bitcast.9) | data formatting | bytes 7340032

commit v7 on v6

--- a/solution.py
+++ b/solution.py
@@ -58,7 +58,7 @@
     B, C, SLOT, NSLOT,
     ids_ref, gates_ref, og_hbm, saved_hbm, wgu_hbm, wd_hbm,
     ig_ref, gg_ref, dg_ref,
-    og_ref, wgu, send, recv, back, Y, GB, XP, RA, RB, GPS, GPR, saved, wT, mt, dpre, dact,
+    og_ref, wgu, send, recv, back, Y, GB, XP, RA, RB, GPS, GPR, saved, wT, early, mt, dpre, dact,
     IDS, TB, sendB, backB, RAB, RBB, selT, perm, permT,
     wsem, ssem, s1s, s1r, ags, agr, gbs, gbr, xps, rar, rbr, gps, gpr, rets, backr,
     idss, idsr, tbs, tbr, sbs, sbr, xpbs, bbr, pbs, rabr, rbbr,
@@ -213,7 +213,7 @@
         if first == 0:
             recv[:PAD] = send[:PAD]
 
-    a_send(0, K // 2)
+    a_send(0, max(1, 3 * K // 4))
     TB[:T] = og_ref[:, DA:]
     for m in range(4):
         mt[m] = picks_t[m]
@@ -385,6 +385,23 @@
             if ROWS > lo:
                 wait_for(XP.at[pl.ds(base + lo, ROWS - lo), colsB], xpbs.at[o])
 
+        def tile_a(i, _):
+            cols = pl.ds(pl.multiple_of(i * WA, TILE), WA)
+            XP[base : base + ROWS, cols] = mm_nt(dpre[...], wgu[cols, :]).astype(BF16)
+            return 0
+
+        lax.fori_loop(0, DA // WA, tile_a, 0)
+
+        cut = cut_of(c)
+        rest = BLK - cut
+
+        def part_of(j, lo, size):
+            return XP.at[pl.ds(base + j * BLK + lo, size), colsA]
+
+        remote(part_of(2, 0, cut), RA.at[c, pl.ds(0, cut)], xps.at[c], rar.at[c, 0], right)
+        remote(part_of(2, cut, rest), RA.at[c, pl.ds(cut, rest)], xps.at[c], rar.at[c, 1], left)
+        remote(part_of(1, cut, rest), RB.at[c, 0, pl.ds(cut, rest)], xps.at[c], rbr.at[c, 0], right)
+        remote(part_of(3, 0, cut), RB.at[c, 1, pl.ds(0, cut)], xps.at[c], rbr.at[c, 1], left)
         def tile_b(i, _):
             cols = pl.ds(pl.multiple_of(DA + i * WB, 128), WB)
             XP[base : base + ROWS, cols] = mm(permT[...], mm_nt(dpre[...], wgu[cols, :]).astype(BF16)).astype(BF16)
@@ -400,23 +417,6 @@
             else:
                 backB[:MB] = XP[base : base + MB, DA:]
 
-        def tile_a(i, _):
-            cols = pl.ds(pl.multiple_of(i * WA, TILE), WA)
-            XP[base : base + ROWS, cols] = mm_nt(dpre[...], wgu[cols, :]).astype(BF16)
-            return 0
-
-        lax.fori_loop(0, DA // WA, tile_a, 0)
-
-        cut = cut_of(c)
-        rest = BLK - cut
-
-        def part_of(j, lo, size):
-            return XP.at[pl.ds(base + j * BLK + lo, size), colsA]
-
-        remote(part_of(2, 0, cut), RA.at[c, pl.ds(0, cut)], xps.at[c], rar.at[c, 0], right)
-        remote(part_of(2, cut, rest), RA.at[c, pl.ds(cut, rest)], xps.at[c], rar.at[c, 1], left)
-        remote(part_of(1, cut, rest), RB.at[c, 0, pl.ds(cut, rest)], xps.at[c], rbr.at[c, 0], right)
-        remote(part_of(3, 0, cut), RB.at[c, 1, pl.ds(0, cut)], xps.at[c], rbr.at[c, 1], left)
         wT[:, c * ROWS : (c + 1) * ROWS] = jnp.transpose(dact[...]).astype(BF16)
 
     def reduce_middle(c):
@@ -502,7 +502,7 @@
     routes = b_routes()
     b_select(0, routes)
     b_select(1, routes)
-    a_send(K // 2, K)
+    a_send(max(1, 3 * K // 4), K)
     gather_start(1)
     gather_forward(0)
     for c in range(2, min(4, K)):
@@ -540,21 +540,35 @@
     b_middle()
     b_end()
 
-    for c in range(K):
-        lo = PAD if c == 0 else 0
-        if MSG > lo:
-            wait_for(back.at[pl.ds(c * MSG + lo, MSG - lo)], backr.at[c])
-    last = jnp.zeros((T, S), F32)
-    for m in range(4):
-        ig_ref[:, segs[m]] = mm(mt[3], back[:, segs[m]]).astype(BF16)
-        if m < 3:
-            last += mm(mt[m], back[:, segs[m]])
-    ig_ref[:, tail] = last.astype(BF16)
-    back_gates = jnp.transpose(back[:, extra].astype(F32)).astype(BF16)
-    for k, (blk, rank) in enumerate(own):
-        at = slots - blk * PAD
-        found = mm(back_gates, hot((at == SLOT) | (at == SLOT + 1)))
-        gg_ref[k : k + 1, :] = jnp.sum(jnp.where(lane_slot == rank, found, 0.0), axis=0, keepdims=True)
+    def own_sums(first, last):
+        for c in range(first, last):
+            lo = PAD if c == 0 else 0
+            if MSG > lo:
+                wait_for(back.at[pl.ds(c * MSG + lo, MSG - lo)], backr.at[c])
+        rows = slice(first * MSG, last * MSG)
+        ends = jnp.zeros((T, S), F32)
+        sums = []
+        for m in range(4):
+            sums.append(mm(mt[3, :, rows], back[rows, segs[m]]))
+            if m < 3:
+                ends += mm(mt[m, :, rows], back[rows, segs[m]])
+        back_gates = jnp.transpose(back[rows, extra].astype(F32)).astype(BF16)
+        found = []
+        for k, (blk, rank) in enumerate(own):
+            at = slots[rows] - blk * PAD
+            chosen = mm(back_gates, hot((at == SLOT) | (at == SLOT + 1)))
+            found.append(jnp.sum(jnp.where(lane_slot == rank, chosen, 0.0), axis=0, keepdims=True))
+        return sums + [ends], found
+
+    first_sums, first_found = own_sums(0, K - 1)
+    for m in range(5):
+        early[:, (segs + [tail])[m]] = first_sums[m]
+    last_sums, last_found = own_sums(K - 1, K)
+    for m in range(5):
+        cols = (segs + [tail])[m]
+        ig_ref[:, cols] = (early[:, cols] + last_sums[m]).astype(BF16)
+    for k in range(2):
+        gg_ref[k : k + 1, :] = first_found[k] + last_found[k]
 
     wait_for(send.at[pl.ds(0, K * MSG - PAD)], s1s)
     wait_for(recv.at[pl.ds(0, K * MSG - PAD)], rets)
@@ -617,6 +631,7 @@
             pltpu.VMEM((K, NX, PAD, 128), BF16),
             pltpu.VMEM((K * ROWS, 2 * H), BF16),
             pltpu.VMEM((H, K * ROWS), BF16),
+            pltpu.VMEM((T, DA), F32),
             pltpu.VMEM((4, T, K * MSG), BF16),
             pltpu.VMEM((ROWS, 2 * H), BF16),
             pltpu.VMEM((ROWS, H), F32),

time: 166 us -> 160 us (0.964)
  Pallas kernels: 162 us -> 155 us
    pallas_call x1, Pallas kernels: 162 us -> 155 us  [body(): pl.pallas_call(functools.partial(kernel, B, C, SLOT, NSLOT), out_shape=(p...]
where the time goes in v7:
time: 160 us; the launch traced here: 159 us
  Pallas kernels  155 us (97%)
  local copies, waits for them, and re-layouts  3.32 us (2%)
    pallas_call x1, Pallas kernels, body(): pl.pallas_call(functools.partial(kernel, B, C, SLOT, NSLOT), out_shape=(p...  155 us
    unnamed x3, local copies, waits for them, and re-layouts  3.32 us

profile of v7, /device:TPU:0, one launch (start us, length us, event | category | flops | bytes accessed | tf_op | source)
XLA Modules:
  0.0 159.4 jit_solution(13363090506933125475)
XLA Ops:
  0.6 155.5 %moe_backward.1 = (bf16[128,3584]{1,0:T(8,128)(2,1)S(1)}, f32[2,128]{1,0:T(2,128)S(1)}, bf16[512,3584]{1,0:T(8,128)(2,1)S(1)}) custom-call(s32[2,128]{1,0:T(2,128)} %bitcast.14, bf16[2,128]{1,0:T(2,128)(2,1)} %bitcast.15, bf16[128,3584]{1,0:T(8,128)(2,1)} %og_hbm.1, bf16[12,128,1024]{2,1,0:T(8,128)(2,1)} %bitcast.13, bf16[3584,1024]{1,0:T(8,128)(2,1)} %bitcast.11, ...), custom_call_target="tpu_custom_call" | custom-call | flops 22548578304 | bytes 25000000 | tf_op jit(solution)/shard_map/moe_backward/pallas_call | solution.py:610
  156.1 0.9 copy.12
  157.0 0.6 copy.13
  157.6 1.8 %copy.14 = bf16[1,512,3584]{2,1,0:T(8,128)(2,1)} copy(bf16[1,512,3584]{2,1,0:T(8,128)(2,1)S(1)} %bitcast.9) | data formatting | bytes 7340032

commit v8 on v7

--- a/solution.py
+++ b/solution.py
@@ -501,8 +501,8 @@
     gather_start(0)
     routes = b_routes()
     b_select(0, routes)
+    a_send(max(1, 3 * K // 4), K)
     b_select(1, routes)
-    a_send(max(1, 3 * K // 4), K)
     gather_start(1)
     gather_forward(0)
     for c in range(2, min(4, K)):

time: 160 us -> 163 us (1.019)
  the two profiles are of different devices: /device:TPU:0 before, /device:TPU:83 now
where the time goes in v8:
time: 163 us
  Pallas kernels  159 us (98%)
  local copies, waits for them, and re-layouts  3.32 us (2%)
    pallas_call x1, Pallas kernels, body(): pl.pallas_call(functools.partial(kernel, B, C, SLOT, NSLOT), out_shape=(p...  159 us
    unnamed x3, local copies, waits for them, and re-layouts  3.32 us

profile of v8, /device:TPU:83, one launch (start us, length us, event | category | flops | bytes accessed | tf_op | source)
XLA Modules:
  0.0 162.9 jit_solution(17292563390871679974)
XLA Ops:
  0.6 159.0 %moe_backward.1 = (bf16[128,3584]{1,0:T(8,128)(2,1)S(1)}, f32[2,128]{1,0:T(2,128)S(1)}, bf16[512,3584]{1,0:T(8,128)(2,1)S(1)}) custom-call(s32[2,128]{1,0:T(2,128)} %bitcast.14, bf16[2,128]{1,0:T(2,128)(2,1)} %bitcast.15, bf16[128,3584]{1,0:T(8,128)(2,1)} %og_hbm.1, bf16[12,128,1024]{2,1,0:T(8,128)(2,1)} %bitcast.13, bf16[3584,1024]{1,0:T(8,128)(2,1)} %bitcast.11, ...), custom_call_target="tpu_custom_call" | custom-call | flops 22548578304 | bytes 25000000 | tf_op jit(solution)/shard_map/moe_backward/pallas_call | solution.py:610
  159.6 0.9 copy.12
  160.5 0.6 copy.13
  161.1 1.8 %copy.14 = bf16[1,512,3584]{2,1,0:T(8,128)(2,1)} copy(bf16[1,512,3584]{2,1,0:T(8,128)(2,1)S(1)} %bitcast.9) | data formatting | bytes 7340032
